TPU v7x, 128 devices: a whole 4x4x4 slice. The times are simulated.
128 devices in a mesh: ka: 4 (over x_hi, core), vert: 32 (over y, x_lo, z).
Axes of the slice: x: 4 (x_hi: 2, x_lo: 2; x = x_hi * 2 + x_lo), y: 4, z: 4, core: 2. Of those that a mesh axis runs over, the one named last changes fastest.
Arguments:
- eig_lower: bfloat16 [512, 65536], P(None, ('ka', 'vert')), may hold values from -6 to 6
- eig_upper: bfloat16 [256, 65536], P(None, ('ka', 'vert')), may hold values from -6 to 6
- layout_map: int32 [65536], replicated, may hold values from 0 to 65535, as said below
- block_live: int32 [8], replicated, may hold values from 1 to 8192, 40960 in all
- coupling: int32 [8, 3], replicated, may hold values 0 or 1
- rot_coef: float32 [8, 3], replicated, may hold values from -4 to 4
- dip_zero: bfloat16 [8192, 8192], P('vert', 'ka'), may hold values from -0.00030517578 to 0.00030517578
- dip_raise: bfloat16 [8192, 8192], P('vert', 'ka'), may hold values from -0.00030517578 to 0.00030517578
- dip_lower: bfloat16 [8192, 8192], P('vert', 'ka'), may hold values from -0.00030517578 to 0.00030517578
Outputs:
- strength: float32 [512, 256], P('ka', 'vert')
Inputs may be any that keep to these rules, and one draw needn't show every extreme that they name: layout_map is a permutation of 0 to 65535 made of runs of 128 solver rows that hold 128 consecutive basis rows beginning at a multiple of 128. The solver rows lie on the devices of ka+vert in runs of 512, in device order; each run holds exactly 128 basis rows of each range of 16384 consecutive basis rows. `block_live`: the sizes sum to 40960; one of them is 8192.
All inputs are finite; a program needn't handle non-finite values.
Results may differ from a plain program's by a relative error of at most 0.0033.
Values may be sent and summed in bfloat16 or wider, within the bound.
A program may use at most 128 MiB of HBM per device.

v0:
```python
import jax
import jax.numpy as jnp
from jax import lax
from jax.sharding import PartitionSpec as P

NV = 8192


def combine_terms(upper_range, mat_zero, mat_raise, mat_lower, factors):
    term_zero = jnp.einsum("fkc,rc->fkr", upper_range, mat_zero, preferred_element_type=jnp.float32)
    term_raise = jnp.einsum(
        "fkc,rc->fkr", upper_range, mat_raise, preferred_element_type=jnp.float32
    )
    term_lower = jnp.einsum(
        "fkc,rc->fkr", upper_range, mat_lower, preferred_element_type=jnp.float32
    )
    edge_zero = jnp.zeros_like(term_zero[:, :1])
    raised = jnp.concatenate([term_raise[:, 1:], edge_zero], axis=1)
    lowered = jnp.concatenate([edge_zero, term_lower[:, :-1]], axis=1)
    return (
        factors[:, 0][None, :, None] * term_zero
        + factors[:, 1][None, :, None] * raised
        + factors[:, 2][None, :, None] * lowered
    )


def per_device(
    eig_lower, eig_upper, layout_map, block_live, coupling, rot_coef, dip_zero, dip_raise, dip_lower
):
    owners = lax.axis_size("ka")
    columns = lax.axis_size("vert")
    devices = owners * columns
    total_rows = layout_map.shape[0]
    owner_rows = total_rows // owners
    local_rows = eig_lower.shape[1]
    owner_slot = local_rows // owners
    run_rows = min(128, owner_slot)
    local_runs = local_rows // run_rows
    owner_runs = owner_rows // run_rows
    device_here = lax.axis_index(("ka", "vert"))
    owner_here = lax.axis_index("ka")
    run_heads = layout_map.reshape(total_rows // run_rows, run_rows)[:, 0]
    local_heads = lax.dynamic_slice_in_dim(run_heads, device_here * local_runs, local_runs)
    send_order = jnp.argsort(local_heads // owner_rows, stable=True)
    send_table = (send_order[:, None] == jnp.arange(local_runs, dtype=jnp.int32)[None, :]).astype(
        jnp.bfloat16
    )

    def pack(vectors):
        count = vectors.shape[0]
        shaped = vectors.reshape(count, local_runs, run_rows)
        picked = jnp.einsum("nob,po->npb", shaped, send_table, preferred_element_type=jnp.float32)
        picked = picked.astype(jnp.bfloat16).reshape(count, local_rows)
        col_width = count // columns
        shaped = picked.reshape(columns, col_width, owners, owner_slot)
        return shaped.transpose(2, 0, 1, 3).reshape(devices, col_width, owner_slot)

    got_lower, got_upper = (
        lax.all_to_all(pack(eig_lower), ("ka", "vert"), split_axis=0, concat_axis=0, tiled=True),
        lax.all_to_all(pack(eig_upper), ("ka", "vert"), split_axis=0, concat_axis=0, tiled=True),
    )
    positions = jnp.nonzero(run_heads // owner_rows == owner_here, size=owner_runs)[0]
    target_runs = (run_heads[positions] - owner_here * owner_rows) // run_rows
    place_table = (jnp.arange(owner_runs, dtype=jnp.int32)[:, None] == target_runs[None, :]).astype(
        jnp.bfloat16
    )
    own_blocks = owner_rows // NV
    live_own = lax.dynamic_slice_in_dim(block_live, owner_here * own_blocks, own_blocks)
    live_mask = jnp.arange(NV, dtype=jnp.int32)[None, :] < live_own[:, None]

    def place(received):
        col_width = received.shape[1]
        in_order = received.transpose(1, 0, 2)
        arranged = jnp.einsum(
            "csb,ts->ctb", in_order, place_table, preferred_element_type=jnp.float32
        )
        arranged = arranged.astype(jnp.bfloat16).reshape(col_width, own_blocks, NV)
        return jnp.where(live_mask[None], arranged, jnp.zeros_like(arranged))

    lower_own = place(got_lower)
    upper_own = place(got_upper)
    factors = rot_coef * coupling.astype(jnp.float32)
    gathered = lax.all_gather(upper_own, "vert", axis=0, tiled=True)
    half_block = combine_terms(
        lax.all_to_all(gathered, "ka", split_axis=2, concat_axis=1, tiled=True),
        dip_zero,
        dip_raise,
        dip_lower,
        factors,
    ).astype(jnp.bfloat16)
    lower_rows = lax.all_to_all(lower_own, "vert", split_axis=2, concat_axis=0, tiled=True)
    lower_all = lax.all_gather(lower_rows, "ka", axis=1, tiled=True)
    amplitude = jnp.einsum("ikr,fkr->if", lower_all, half_block, preferred_element_type=jnp.float32)
    partial_sum = lax.psum_scatter(amplitude, "vert", scatter_dimension=1, tiled=True)
    summed = lax.psum_scatter(partial_sum, "ka", scatter_dimension=0, tiled=True)
    return summed * summed


def solution(mesh):
    return jax.shard_map(
        per_device,
        mesh=mesh,
        in_specs=(
            P(None, ("ka", "vert")),
            P(None, ("ka", "vert")),
            P(),
            P(),
            P(),
            P(),
            P("vert", "ka"),
            P("vert", "ka"),
            P("vert", "ka"),
        ),
        out_specs=P("ka", "vert"),
        check_vma=False,
    )
```

profile of v0, /device:TPU:1, one launch (start us, length us, event | category | flops | bytes accessed | tf_op | source)
XLA Modules:
  0.0 578.2 jit_solution(390717609736808022)
XLA Ops:
  7.4 0.0 copy-start
  7.4 1.2 slice_reduce_fusion.1
  8.6 0.1 dynamic-slice_reduce_fusion
  8.7 1.0 reshape.181
  9.8 0.7 sort.17
  10.5 0.3 convolution_convert_fusion.3
  10.9 0.7 copy.41
  11.6 11.5 %all-to-all-start.2 = ((bf16[128,8,128]{2,1,0:T(8,128)(2,1)}), bf16[128,8,128]{2,1,0:T(8,128)(2,1)S(1)}, u32[]{:S(2)}, u32[]{:S(2)}) async-start(bf16[128,8,128]{2,1,0:T(8,128)(2,1)} %bitcast.19), calls=%async_computation.2 | async-start | bytes 524288 | tf_op jit(solution)/shard_map/all_to_all | solution.py:60
  23.1 0.0 all-gather.5.cloned.1.call-start
  23.2 0.6 convert_reduce_fusion
  23.8 0.3 reduce-window.12
  24.1 0.1 slice.26
  24.2 0.1 slice_reduce_fusion
  24.3 0.1 broadcast_add_fusion
  24.4 4.1 scatter_custom_fusion
  28.5 0.1 copy.35
  28.6 0.2 select_n.91
  28.8 0.7 dynamic_slice.8
  29.5 0.7 iota_compare_fusion
  30.2 0.8 fusion.15
  31.0 1.3 gather_fusion
  32.3 1.4 copy.40
  33.6 0.6 all-to-all-done.2
  34.3 0.2 fusion.1
  34.5 0.1 reshape.183
  34.5 1.0 broadcast_select_fusion.1
  35.5 0.0 all-gather.5.cloned.1.call-update
  35.5 0.0 copy-done.2
  35.5 0.1 reshape.178
  35.7 0.5 convolution_convert_fusion
  36.2 0.1 copy.36
  36.2 25.0 %all_to_all.46 = bf16[128,16,128]{2,1,0:T(8,128)(2,1)S(1)} all-to-all(bf16[128,16,128]{2,1,0:T(8,128)(2,1)S(1)} %bitcast.95), channel_id=1, replica_groups=mesh['ka'=4,'vert'=32] {'ka','vert'}, dimensions={0} | all-to-all | bytes 1048576 | tf_op jit(solution)/shard_map/all_to_all | solution.py:59
  61.3 0.3 fusion
  61.6 0.1 reshape.180
  61.7 6.8 %copy.38 = bf16[16,2,8192]{0,1,2:T(2,128)(2,1)} copy(bf16[16,2,8192]{2,1,0:T(2,128)(2,1)S(1)} %reshape.180) | data formatting | bytes 1048576 | tf_op jit(solution)/shard_map/reshape | solution.py:77
  68.5 26.6 %fusion.37 = bf16[8192,2,16]{2,1,0:T(2,128)(2,1)} fusion(bf16[16,2,8192]{0,1,2:T(2,128)(2,1)} %copy.38, pred[2,8192]{0,1:T(8,128)(4,1)S(1)} %iota_compare_fusion), kind=kLoop, calls=%fused_computation.79 | loop fusion | flops 262144 | bytes 1064960
  95.1 12.9 %reshape.213 = bf16[32,2,4096]{2,1,0:T(2,128)(2,1)} reshape(bf16[8192,2,16]{2,1,0:T(2,128)(2,1)} %fusion.37) | data formatting | bytes 1048576
  108.0 5.3 all-to-all-start.1
  113.3 79.0 %all-gather.5.cloned.1.call-done = bf16[256,2,8192]{2,1,0:T(2,128)(2,1)} async-done(((bf16[8,2,8192]{2,1,0:T(2,128)(2,1)}), bf16[256,2,8192]{2,1,0:T(2,128)(2,1)}) %all-gather.5.cloned.1.call-update) | async-done | bytes 8388624 | tf_op jit(solution)/shard_map/all_gather | solution.py:83
  192.3 28.6 %copy.43 = bf16[256,2,8192]{0,1,2:T(2,128)(2,1)} copy(bf16[256,2,8192]{2,1,0:T(2,128)(2,1)} %all-gather.5.cloned.1.call-done) | data formatting | bytes 16777216 | tf_op jit(solution)/shard_map/all_gather | solution.py:83
  220.9 0.0 all-to-all-done.1
  220.9 25.0 %all-to-all-start.3 = ((bf16[256,2,8192]{0,1,2:T(2,128)(2,1)}), bf16[256,2,8192]{0,1,2:T(2,128)(2,1)}, u32[]{:S(2)}, u32[]{:S(2)}) async-start(bf16[256,2,8192]{0,1,2:T(2,128)(2,1)} %copy.43), calls=%async_computation.3 | async-start | bytes 16777216 | tf_op jit(solution)/shard_map/all_to_all | solution.py:85
  245.9 0.0 all-gather.3.cloned.1.call-start
  245.9 4.1 reshape.214
  250.0 9.4 %copy.39 = bf16[32,16,2,256]{3,1,0,2:T(8,128)(2,1)} copy(bf16[32,16,2,256]{1,2,3,0:T(2,128)(2,1)} %bitcast.89) | data formatting | bytes 1048576 | tf_op jit(solution)/shard_map/all_to_all | solution.py:91
  259.4 0.0 all-gather.3.cloned.1.call-update
  259.4 0.0 reduce-scatter.3.cloned.1.call-start
  259.4 0.0 copy-done.3
  259.5 0.0 copy-done.4
  259.5 90.9 %all-to-all-done.3 = bf16[256,2,8192]{0,1,2:T(2,128)(2,1)} async-done(((bf16[256,2,8192]{0,1,2:T(2,128)(2,1)}), bf16[256,2,8192]{0,1,2:T(2,128)(2,1)}, u32[]{:S(2)}, u32[]{:S(2)}) %all-to-all-start.3) | async-done | bytes 8388640 | tf_op jit(solution)/shard_map/all_to_all | solution.py:85
  350.4 7.7 %copy.44 = bf16[256,2,8192]{0,2,1:T(8,128)(2,1)} copy(bf16[256,2,8192]{0,1,2:T(2,128)(2,1)} %all-to-all-done.3) | data formatting | bytes 16777216 | tf_op jit(solution)/shard_map/all_to_all | solution.py:85
  358.0 11.6 %copy.45 = bf16[256,4,2,2048]{3,0,2,1:T(8,128)(2,1)} copy(bf16[256,4,2,2048]{0,3,1,2:T(8,128)(2,1)} %bitcast.88) | data formatting | bytes 16777216 | tf_op jit(solution)/shard_map/all_to_all | solution.py:85
  369.6 0.0 copy-done
  369.6 6.7 %fusion.2 = f32[256,7,256]{2,0,1:T(8,128)} fusion(bf16[256,8,2048]{2,0,1:T(8,128)(2,1)} %bitcast.90, bf16[256,2048]{1,0:T(8,128)(2,1)S(1)} %copy-done), kind=kOutput, calls=%fused_computation.12 | convolution fusion | flops 1879048192 | bytes 11272192 | tf_op jit(solution)/shard_map/slice | solution.py:19
  376.3 0.0 copy-done.1
  376.3 3.4 fusion.4
  379.7 0.0 copy-done.6
  379.7 9.5 %convolution_bitcast_fusion = f32[512,256]{0,1:T(8,128)} fusion(bf16[512,8,256]{2,0,1:T(8,128)(2,1)} %all-gather.3.cloned.1.call-done, f32[256,7,256]{2,0,1:T(8,128)} %fusion.2, f32[256,7,256]{2,0,1:T(8,128)} %fusion.4, bf16[256,8,2048]{2,0,1:T(8,128)(2,1)} %bitcast.91, bf16[256,2048]{1,0:T(8,128)(2,1)S(1)} %copy-done.6, f32[8]{0:T(128)S(1)} %get-tuple-element.10, ...), kind=kOutput, calls=%fused_computation.8 | convolution fusion | flops 2687500288 | bytes 15728736 | tf_op jit(solution)/shard_map/ikr,fkr->if/dot_general | solution.py:93
  389.2 0.0 reduce-scatter.3.cloned.1.call-update
  389.2 0.0 reduce-scatter.5.cloned.1.call-start
  389.2 132.9 %reduce-scatter.3.cloned.1.call-done = f32[512,8]{0,1:T(8,128)} async-done(((f32[512,256]{0,1:T(8,128)}), f32[512,8]{0,1:T(8,128)}) %reduce-scatter.3.cloned.1.call-update) | async-done | bytes 16400 | tf_op jit(solution)/shard_map/reduce_scatter | solution.py:94
  522.1 0.0 reduce-scatter.5.cloned.1.call-update
  522.1 47.3 %reduce-scatter.5.cloned.1.call-done = f32[128,8]{0,1:T(8,128)} async-done(((f32[512,8]{0,1:T(8,128)}), f32[128,8]{0,1:T(8,128)}) %reduce-scatter.5.cloned.1.call-update) | async-done | bytes 4112 | tf_op jit(solution)/shard_map/reduce_scatter | solution.py:95
  569.5 1.3 mul.62
  (18 shorter events, 0.1 us)
Async XLA Ops:
  7.4 362.2 %copy-start = (bf16[256,2048]{1,0:T(8,128)(2,1)S(1)}, bf16[256,2048]{1,0:T(8,128)(2,1)}, u32[]{:S(2)}) copy-start(bf16[256,2048]{1,0:T(8,128)(2,1)} %param.17) | copy-start | bytes 3145732
  7.4 28.2 %copy-start.2 = (bf16[512,512]{1,0:T(8,128)(2,1)S(1)}, bf16[512,512]{1,0:T(8,128)(2,1)}, u32[]{:S(2)}) copy-start(bf16[512,512]{1,0:T(8,128)(2,1)} %param.9) | copy-start | bytes 1572868
  11.6 22.7 %all-to-all-start.2 = ((bf16[128,8,128]{2,1,0:T(8,128)(2,1)}), bf16[128,8,128]{2,1,0:T(8,128)(2,1)S(1)}, u32[]{:S(2)}, u32[]{:S(2)}) async-start(bf16[128,8,128]{2,1,0:T(8,128)(2,1)} %bitcast.19), calls=%async_computation.2 | async-start | bytes 524288 | tf_op jit(solution)/shard_map/all_to_all | solution.py:60
  23.1 169.2 %all-gather.5.cloned.1.call-start = ((), (), s32[]{:S(2)}) async-start(), calls=%async_computation.7 | async-start | bytes 8650752 | tf_op jit(solution)/shard_map/all_gather | solution.py:83
  108.0 112.9 %all-to-all-start.1 = ((bf16[32,2,4096]{2,1,0:T(2,128)(2,1)}), bf16[32,2,4096]{2,1,0:T(2,128)(2,1)S(1)}, u32[]{:S(2)}, u32[]{:S(2)}) async-start(bf16[32,2,4096]{2,1,0:T(2,128)(2,1)} %reshape.213), calls=%async_computation.1 | async-start | bytes 1048576 | tf_op jit(solution)/shard_map/all_to_all | solution.py:91
  220.9 129.5 %all-to-all-start.3 = ((bf16[256,2,8192]{0,1,2:T(2,128)(2,1)}), bf16[256,2,8192]{0,1,2:T(2,128)(2,1)}, u32[]{:S(2)}, u32[]{:S(2)}) async-start(bf16[256,2,8192]{0,1,2:T(2,128)(2,1)} %copy.43), calls=%async_computation.3 | async-start | bytes 16777216 | tf_op jit(solution)/shard_map/all_to_all | solution.py:85
  245.9 13.6 %copy-start.3 = (f32[8,3]{0,1:T(4,128)S(1)}, f32[8,3]{0,1:T(4,128)}, u32[]{:S(2)}) copy-start(f32[8,3]{0,1:T(4,128)} %param.14) | copy-start | bytes 292
  245.9 13.6 %copy-start.4 = (s32[8,3]{0,1:T(4,128)S(1)}, s32[8,3]{0,1:T(4,128)}, u32[]{:S(2)}) copy-start(s32[8,3]{0,1:T(4,128)} %param.13) | copy-start | bytes 292
  245.9 133.9 %all-gather.3.cloned.1.call-start = ((), (), s32[]{:S(2)}) async-start(), calls=%async_computation.6 | async-start | bytes 2621440 | tf_op jit(solution)/shard_map/all_gather | solution.py:92
  259.4 262.7 %reduce-scatter.3.cloned.1.call-start = ((), (), s32[]{:S(2)}) async-start(), calls=%async_computation.8 | async-start | bytes 540672 | tf_op jit(solution)/shard_map/reduce_scatter | solution.py:94
  369.6 6.7 %copy-start.1 = (bf16[256,4,2,2048]{3,0,2,1:T(8,128)(2,1)S(1)}, bf16[256,4,2,2048]{3,0,2,1:T(8,128)(2,1)}, u32[]{:S(2)}) copy-start(bf16[256,4,2,2048]{3,0,2,1:T(8,128)(2,1)} %copy.45) | copy-start | bytes 25165828
  369.6 6.7 %copy-start.5 = (bf16[256,2048]{1,0:T(8,128)(2,1)S(1)}, bf16[256,2048]{1,0:T(8,128)(2,1)}, u32[]{:S(2)}) copy-start(bf16[256,2048]{1,0:T(8,128)(2,1)} %param.16) | copy-start | bytes 3145732
  376.3 3.4 copy-start.6
  389.2 180.3 %reduce-scatter.5.cloned.1.call-start = ((), (), s32[]{:S(2)}) async-start(), calls=%async_computation.9 | async-start | bytes 20480 | tf_op jit(solution)/shard_map/reduce_scatter | solution.py:95
Sparse Core Ops, SparseCore 0:
  35.7 156.5 all-gather.4
  389.3 132.7 reduce-scatter.2
Sparse Core Ops, SparseCore 1:
  259.5 37.7 all-gather.2
  522.2 47.2 reduce-scatter.4
where the time goes:
time: 580 us; the launch traced here: 578 us
  waiting for transfers between devices  351 us (61%)
  local copies, waits for them, and re-layouts  88.2 us (15%)
  starting transfers between devices  41.9 us (7%)
  other arithmetic  36.4 us (6%)
  blocking collectives  25 us (4%)
  matrix products  20.9 us (4%)
  between operations  15 us (3%)
    reduce_scatter x1, waiting for transfers between devices, per_device(): lax.psum_scatter(amplitude, 'vert', scatter_dimension=1, tiled=True)  133 us
    all_to_all x1, waiting for transfers between devices, per_device(): lax.all_to_all(gathered, 'ka', split_axis=2, concat_axis=1, tiled=True)  90.9 us
    all_gather x1, waiting for transfers between devices, per_device(): gathered = lax.all_gather(upper_own, 'vert', axis=0, tiled=True)  79 us
    reduce_scatter x1, waiting for transfers between devices, per_device(): lax.psum_scatter(partial_sum, 'ka', scatter_dimension=0, tiled=True)  47.3 us
    all_gather x1, local copies, waits for them, and re-layouts, per_device(): gathered = lax.all_gather(upper_own, 'vert', axis=0, tiled=True)  28.6 us
    unnamed x1, other arithmetic  26.6 us
    all_to_all x1, blocking collectives, per_device(): lax.all_to_all(pack(eig_lower), ('ka', 'vert'), split_axis=0, concat_axis...  25 us
    all_to_all x1, starting transfers between devices, per_device(): lax.all_to_all(gathered, 'ka', split_axis=2, concat_axis=1, tiled=True)  25 us
  transfers between devices with their start and end apart: 7, of which 5 were waited for; matrix products, arithmetic and copies ran while one was open for 22% of the time, Pallas kernels for 0%

commit v1 on v0

v1 whole, which is shorter than its diff:
```python
import jax
import jax.numpy as jnp
from jax import lax
from jax.experimental import pallas as pl
from jax.experimental.pallas import tpu as pltpu
from jax.sharding import PartitionSpec as P

F32 = jnp.float32
BF16 = jnp.bfloat16
MESH = pl.DeviceIdType.MESH
WIDTHS = (768, 768, 256, 256)
STARTS = (0, 768, 1536, 1792)
ORDERS = ("xyz", "xzy", "yzx", "zyx")
NT = (((1,), (1,)), ((), ()))


def kernel(
    head_ref, src_ref, live_ref, coup_ref, rot_ref, low_ref, up_ref, dz_hbm, dr_hbm, dl_hbm,
    out_ref,
    send_buf, recv_buf, sta, stb, stc, std_, ua, ub, uc, ud, stage_low, low_all, dip, half, amp, parts,
    dip_sem, a_send, a_recv, q_send, q_recv, g_send, g_recv, l_send, l_recv, m_send, m_recv, r_send, r_recv,
):
    ka = lax.axis_index("ka")
    vert = lax.axis_index("vert")
    me = ka * 32 + vert
    yy = vert // 8
    xx = (vert // 4) % 2
    zz = vert % 4
    stages = (sta, stb, stc, std_)
    uppers = (ua, ub, uc, ud)

    barrier = pltpu.get_barrier_semaphore()

    def greet(k, _):
        pl.semaphore_signal(
            barrier, inc=1, device_id=((ka + k // 32) % 4, (vert + k % 32) % 32), device_id_type=MESH
        )
        return 0

    lax.fori_loop(1, 128, greet, 0)
    dips = [pltpu.make_async_copy(h, dip.at[n], dip_sem.at[n]) for n, h in enumerate((dz_hbm, dr_hbm, dl_hbm))]
    for c in dips:
        c.start()

    lane = lax.broadcasted_iota(jnp.int32, (8, 128), 1)
    zeros = jnp.zeros((8, 128), jnp.int32)
    heads = [zeros + head_ref[me * 4 + r] for r in range(4)]
    owned = [[(heads[r] >= o * 128) & (heads[r] < (o + 1) * 128) for r in range(3)] for o in range(4)]

    def pack(j, _):
        for u in range(3):
            unit = up_ref[j] if u == 0 else low_ref[2 * j + u - 1]
            runs = [unit[:, r * 128:(r + 1) * 128].astype(F32) for r in range(4)]
            for o in range(4):
                value = runs[3]
                for r in range(3):
                    value = jnp.where(owned[o][r], runs[r], value)
                send_buf[o * 32 + j, u] = value.astype(BF16)
        return 0

    lax.fori_loop(0, 32, pack, 0)
    pl.semaphore_wait(barrier, 127)

    def spread(k, _):
        ka2, v2 = (ka + k // 32) % 4, (vert + k % 32) % 32
        pltpu.make_async_remote_copy(
            src_ref=send_buf.at[ka2 * 32 + v2], dst_ref=recv_buf.at[me],
            send_sem=a_send, recv_sem=a_recv, device_id=(ka2, v2), device_id_type=MESH,
        ).start()
        return 0

    lax.fori_loop(1, 128, spread, 0)
    recv_buf[me] = send_buf[me]
    pltpu.make_async_copy(recv_buf.at[pl.ds(0, 127)], recv_buf.at[pl.ds(0, 127)], a_recv).wait()

    lives = [live_ref[2 * ka + b] for b in range(2)]

    def arrange_up(q, _):
        for n in range(16):
            block = q * 16 + n
            halves = []
            for b in range(2):
                s = src_ref[ka * 128 + b * 64 + block]
                tile = recv_buf[s, 0].astype(F32)
                halves.append(jnp.where(lane + block * 128 < lives[b], tile, 0.0))
            both = jnp.concatenate(halves, axis=0).astype(BF16)
            for c in range(4):
                if STARTS[c] <= n * 128 < STARTS[c] + WIDTHS[c]:
                    at = n * 128 - STARTS[c]
                    stages[c][q, :, at:at + 128] = both
        return 0

    lax.fori_loop(0, 4, arrange_up, 0)

    exchanges = []
    for c in range(4):
        row = []
        for d in range(1, 4):
            q = (ka + d) % 4
            copy = pltpu.make_async_remote_copy(
                src_ref=stages[c].at[q], dst_ref=uppers[c].at[yy, xx, zz, ka],
                send_sem=q_send.at[c, d - 1], recv_sem=q_recv.at[c, d - 1],
                device_id=(q, vert), device_id_type=MESH,
            )
            copy.start()
            row.append(copy)
        exchanges.append(row)
        uppers[c][yy, xx, zz, ka] = stages[c][ka]

    def arrange_low(v, _):
        for b in range(2):
            for h in range(2):
                block = 2 * v + h
                s = src_ref[ka * 128 + b * 64 + block]
                keep = lane + block * 128 < lives[b]
                both = jnp.concatenate(
                    [jnp.where(keep, recv_buf[s, u].astype(F32), 0.0) for u in (1, 2)], axis=0
                ).astype(BF16)
                at = b * 256 + h * 128
                stage_low[v, :, at:at + 128] = both
        return 0

    lax.fori_loop(0, 32, arrange_low, 0)

    def spread_low(k, _):
        v2 = (vert + k) % 32
        pltpu.make_async_remote_copy(
            src_ref=stage_low.at[v2], dst_ref=low_all.at[ka, vert],
            send_sem=l_send, recv_sem=l_recv, device_id=(ka, v2), device_id_type=MESH,
        ).start()
        return 0

    lax.fori_loop(1, 32, spread_low, 0)
    low_all[ka, vert] = stage_low[vert]

    def vid(y, x, z):
        return y * 8 + x * 4 + z

    sent = []

    def chain(c):
        u = uppers[c]
        where = {"y": yy, "x": xx, "z": zz}
        have = {"y": False, "x": False, "z": False}
        count = 0

        def region(fixed):
            idx = []
            for name, size in (("y", 4), ("x", 2), ("z", 4)):
                if name in fixed:
                    idx.append(fixed[name])
                elif have[name]:
                    idx.append(pl.ds(0, size))
                else:
                    idx.append(where[name])
            return u.at[tuple(idx)]

        def go(ref, axis, step):
            nonlocal count
            size = 2 if axis == "x" else 4
            to = dict(where)
            to[axis] = (where[axis] + step) % size
            copy = pltpu.make_async_remote_copy(
                src_ref=ref, dst_ref=ref, send_sem=g_send.at[c, count], recv_sem=g_recv.at[c, count],
                device_id=(ka, vid(to["y"], to["x"], to["z"])), device_id_type=MESH,
            )
            count += 1
            copy.start()
            sent.append(copy)
            return copy

        for axis in ORDERS[c]:
            here = where[axis]
            if axis == "x":
                one = go(region({"x": here}), "x", 1)
                yield
                one.wait_recv()
            else:
                plus = go(region({axis: here}), axis, 1)
                minus = go(region({axis: here}), axis, 3)
                yield
                before, after = (here + 3) % 4, (here + 1) % 4
                other = "z" if axis == "y" else "y"
                if have[other]:
                    first, second = {other: pl.ds(0, 2)}, {other: pl.ds(2, 2)}
                    cut = None
                elif have["x"]:
                    first, second = {"x": 0}, {"x": 1}
                    cut = None
                else:
                    first, second = {}, {}
                    cut = True
                plus.wait_recv()
                r1 = region({axis: before, **first})
                on1 = go(r1.at[pl.ds(0, 2)] if cut else r1, axis, 1)
                minus.wait_recv()
                r2 = region({axis: after, **second})
                on2 = go(r2.at[pl.ds(2, 2)] if cut else r2, axis, 3)
                yield
                on1.wait_recv()
                on2.wait_recv()
            have[axis] = True

    chains = [chain(c) for c in range(4)]

    def low_copy(slot, owner, to):
        return pltpu.make_async_remote_copy(
            src_ref=low_all.at[owner], dst_ref=low_all.at[owner],
            send_sem=m_send.at[slot], recv_sem=m_recv.at[slot], device_id=(to, vert), device_id_type=MESH,
        )

    sibling = (ka // 2) * 2 + (ka + 1) % 2
    across = (ka + 2) % 4
    moves = []
    for c in range(4):
        for copy in exchanges[c]:
            copy.wait_recv()
        next(chains[c])
    for c in (2, 3, 0, 1):
        next(chains[c])
    pltpu.make_async_copy(low_all.at[0, pl.ds(0, 31)], low_all.at[0, pl.ds(0, 31)], l_recv).wait()
    moves.append(low_copy(0, ka, sibling))
    moves.append(low_copy(1, ka, across))
    for m in moves:
        m.start()
    for c in (2, 3, 0, 1):
        next(chains[c])
    for c in (2, 3, 0, 1):
        next(chains[c])
    moves[1].wait_recv()
    moves.append(low_copy(2, across, sibling))
    moves[2].start()
    live_chains = [2, 3, 0, 1]
    while live_chains:
        for c in list(live_chains):
            if next(chains[c], "end") == "end":
                live_chains.remove(c)
    moves[0].wait_recv()
    moves[2].wait_recv()
    for c in dips:
        c.wait()

    def factor(k, d):
        return rot_ref[k, d] * coup_ref[k, d].astype(F32)

    def step(g, _):
        y, x = g // 2, g % 2
        sums = []
        for n in range(3):
            total = None
            for c in range(4):
                rows = uppers[c][y, x].reshape(256, WIDTHS[c])
                term = lax.dot_general(
                    rows, dip[n, :, STARTS[c]:STARTS[c] + WIDTHS[c]], NT, preferred_element_type=F32
                )
                total = term if total is None else total + term
            sums.append(total.reshape(4, 8, 8, 256))
        zero, up, down = sums
        rows = pl.ds(pl.multiple_of(g * 32, 32), 32)
        for k in range(8):
            value = factor(k, 0) * zero[:, k]
            if k < 7:
                value = value + factor(k, 1) * up[:, k + 1]
            if k > 0:
                value = value + factor(k, 2) * down[:, k - 1]
            half[rows, k * 256:(k + 1) * 256] = value.reshape(32, 256).astype(BF16)
        return 0

    lax.fori_loop(0, 8, step, 0)

    for t in range(4):
        total = None
        for o in range(4):
            lows = low_all[o, pl.ds(t * 8, 8)].reshape(128, 512)
            term = lax.dot_general(half[:, o * 512:(o + 1) * 512], lows, NT, preferred_element_type=F32)
            total = term if total is None else total + term
        amp[t] = total.reshape(32, 8, 128)

    def give(k, _):
        ka2, v2 = (ka + k // 32) % 4, (vert + k % 32) % 32
        pltpu.make_async_remote_copy(
            src_ref=amp.at[ka2, v2], dst_ref=parts.at[me],
            send_sem=r_send, recv_sem=r_recv, device_id=(ka2, v2), device_id_type=MESH,
        ).start()
        return 0

    lax.fori_loop(1, 128, give, 0)
    parts[me] = amp[ka, vert]
    pltpu.make_async_copy(parts.at[pl.ds(0, 127)], parts.at[pl.ds(0, 127)], r_recv).wait()
    total = jnp.sum(parts[...], axis=0)
    out_ref[...] = total * total

    pltpu.make_async_copy(send_buf.at[pl.ds(0, 127)], send_buf.at[pl.ds(0, 127)], a_send).wait()
    for row in exchanges:
        for copy in row:
            copy.wait_send()
    pltpu.make_async_copy(stage_low.at[pl.ds(0, 31)], stage_low.at[pl.ds(0, 31)], l_send).wait()
    for copy in sent + moves:
        copy.wait_send()
    pltpu.make_async_copy(parts.at[pl.ds(0, 127)], parts.at[pl.ds(0, 127)], r_send).wait()


def per_device(
    eig_lower, eig_upper, layout_map, block_live, coupling, rot_coef, dip_zero, dip_raise, dip_lower
):
    heads = layout_map.reshape(512, 128)[:, 0] // 128
    hits = heads[None, :] == jnp.arange(512, dtype=jnp.int32)[:, None]
    source = jnp.sum(jnp.where(hits, (jnp.arange(512, dtype=jnp.int32) // 4)[None, :], 0), axis=1)
    smem = pl.BlockSpec(memory_space=pltpu.SMEM)
    vmem = pl.BlockSpec(memory_space=pltpu.VMEM)
    hbm = pl.BlockSpec(memory_space=pl.ANY)
    dma = pltpu.SemaphoreType.DMA
    out = pl.pallas_call(
        kernel,
        out_shape=jax.ShapeDtypeStruct((8, 128), F32),
        in_specs=[smem] * 5 + [vmem] * 2 + [hbm] * 3,
        out_specs=vmem,
        scratch_shapes=[
            pltpu.VMEM((128, 3, 8, 128), BF16),
            pltpu.VMEM((128, 3, 8, 128), BF16),
            *[pltpu.VMEM((4, 16, w), BF16) for w in WIDTHS],
            *[pltpu.VMEM((4, 2, 4, 4, 16, w), BF16) for w in WIDTHS],
            pltpu.VMEM((32, 16, 512), BF16),
            pltpu.VMEM((4, 32, 16, 512), BF16),
            pltpu.VMEM((3, 256, 2048), BF16),
            pltpu.VMEM((256, 2048), BF16),
            pltpu.VMEM((4, 32, 8, 128), F32),
            pltpu.VMEM((128, 8, 128), F32),
            dma((3,)),
            dma, dma,
            dma((4, 3)), dma((4, 3)),
            dma((4, 9)), dma((4, 9)),
            dma, dma,
            dma((3,)), dma((3,)),
            dma, dma,
        ],
        compiler_params=pltpu.CompilerParams(
            collective_id=0, has_side_effects=True, vmem_limit_bytes=48 * 1024 * 1024
        ),
        cost_estimate=pl.CostEstimate(flops=7_000_000_000, bytes_accessed=5_000_000, transcendentals=0),
    )(
        heads, source, block_live, coupling, rot_coef,
        eig_lower.reshape(64, 8, 512), eig_upper.reshape(32, 8, 512), dip_zero, dip_raise, dip_lower,
    )
    return out.T


def solution(mesh):
    return jax.shard_map(
        per_device,
        mesh=mesh,
        in_specs=(
            P(None, ("ka", "vert")),
            P(None, ("ka", "vert")),
            P(),
            P(),
            P(),
            P(),
            P("vert", "ka"),
            P("vert", "ka"),
            P("vert", "ka"),
        ),
        out_specs=P("ka", "vert"),
        check_vma=False,
    )
```

time: 580 us -> 110 us (0.19)
  waiting for transfers between devices: 351 us -> 0 us
  Pallas kernels: 0 us -> 101 us
  local copies, waits for them, and re-layouts: 88.2 us -> 8.27 us
  starting transfers between devices: 41.9 us -> 0 us
  other arithmetic: 36.4 us -> 0.2 us
  blocking collectives: 25 us -> 0 us
  matrix products: 20.9 us -> 0 us
  between operations: 15 us -> 0.03 us
    reduce_scatter x2 -> x0, waiting for transfers between devices: 180 us -> none  [the longest x1 133 us: per_device(): lax.psum_scatter(amplitude, 'vert', scatter_dimension=1, tiled=True)]
    pallas_call x0 -> x1, Pallas kernels: none -> 101 us  [per_device(): pl.pallas_call(kernel, out_shape=jax.ShapeDtypeStruct((8, 128), F32), in_...]
    all_to_all x3 -> x0, waiting for transfers between devices: 91.5 us -> none  [the longest x1 90.9 us: per_device(): lax.all_to_all(gathered, 'ka', split_axis=2, concat_axis=1, tiled=True)]
    all_gather x2 -> x0, waiting for transfers between devices: 79 us -> none  [the longest x1 79 us: per_device(): gathered = lax.all_gather(upper_own, 'vert', axis=0, tiled=True)]
    all_to_all x3 -> x0, starting transfers between devices: 41.8 us -> none  [the longest x1 25 us: per_device(): lax.all_to_all(gathered, 'ka', split_axis=2, concat_axis=1, tiled=True)]
    all_to_all x3 -> x0, local copies, waits for them, and re-layouts: 28.6 us -> none  [the longest x2 19.2 us: per_device(): lax.all_to_all(gathered, 'ka', split_axis=2, concat_axis=1, tiled=True)]
    all_gather x1 -> x0, local copies, waits for them, and re-layouts: 28.6 us -> none  [per_device(): gathered = lax.all_gather(upper_own, 'vert', axis=0, tiled=True)]
    unnamed x1 -> x0, other arithmetic: 26.6 us -> none
  transfers between devices with their start and end apart: 7 -> 0, of which waited for: 5 -> 0; matrix products, arithmetic and copies ran while one was open for 22% -> 0% of each run, Pallas kernels for 0% -> 0%
where the time goes in v1:
time: 110 us; the launch traced here: 109 us
  Pallas kernels  101 us (92%)
  local copies, waits for them, and re-layouts  8.27 us (8%)
    pallas_call x1, Pallas kernels, per_device(): pl.pallas_call(kernel, out_shape=jax.ShapeDtypeStruct((8, 128), F32), in_...  101 us
    unnamed x19, local copies, waits for them, and re-layouts  7.14 us

profile of v1, /device:TPU:1, one launch (start us, length us, event | category | flops | bytes accessed | tf_op | source)
XLA Modules:
  0.0 109.3 jit_solution(7475779461696536998)
XLA Ops:
  0.0 0.0 copy-start.4
  0.0 1.1 %slice_reduce_fusion = s32[512]{0:T(512)S(1)} fusion(s32[512,128]{1,0:T(8,128)} %bitcast.7), kind=kLoop, calls=%fused_computation.2 | loop fusion | bytes 4096 | tf_op jit(solution)/shard_map/slice | solution.py:306
  1.2 0.0 copy-start.6
  1.2 0.2 select_reduce_fusion.src_ref
  1.4 0.5 copy-done.6
  1.8 0.0 copy-start.7
  1.8 0.1 copy.16.coup_ref
  1.9 0.6 copy-done.7
  2.5 0.0 copy-start.5
  2.5 0.1 copy.17.rot_ref
  2.6 0.0 copy-done.4
  2.6 0.6 copy-done.5
  3.2 0.0 copy-start
  3.2 1.2 %copy-done = bf16[256,2048]{1,0:T(8,128)(2,1)S(1)} copy-done((bf16[256,2048]{1,0:T(8,128)(2,1)S(1)}, bf16[256,2048]{1,0:T(8,128)(2,1)}, u32[]{:S(2)}) %copy-start) | copy-done | bytes 1048600
  4.4 0.0 copy-start.1
  4.4 1.2 %copy-done.1 = bf16[256,2048]{1,0:T(8,128)(2,1)S(1)} copy-done((bf16[256,2048]{1,0:T(8,128)(2,1)S(1)}, bf16[256,2048]{1,0:T(8,128)(2,1)}, u32[]{:S(2)}) %copy-start.1) | copy-done | bytes 1048600
  5.6 0.0 copy-start.2
  5.6 1.2 %copy-done.2 = bf16[256,2048]{1,0:T(8,128)(2,1)S(1)} copy-done((bf16[256,2048]{1,0:T(8,128)(2,1)S(1)}, bf16[256,2048]{1,0:T(8,128)(2,1)}, u32[]{:S(2)}) %copy-start.2) | copy-done | bytes 1048600
  6.9 0.0 copy-start.3
  6.9 1.0 copy-done.3
  7.9 100.8 %shard_map.91 = f32[8,128]{1,0:T(8,128)S(1)} custom-call(s32[512]{0:T(512)S(1)} %get-tuple-element.6.head_ref, s32[512]{0:T(512)S(1)} %select_reduce_fusion.src_ref, s32[8]{0:T(128)S(1)} %copy-done.5, s32[8,3]{1,0:T(8,128)S(1)} %copy.16.coup_ref, f32[8,3]{1,0:T(8,128)S(1)} %copy.17.rot_ref, bf16[64,8,512]{2,1,0:T(8,128)(2,1)S(1)} %bitcast.5, ...), custom_call_target="tpu_custom_call" | custom-call | flops 7000000000 | bytes 5000000 | tf_op jit(solution)/shard_map/pallas_call | solution.py:313
  108.7 0.6 copy.19
  (1 shorter events, 0.0 us)
Async XLA Ops:
  0.0 2.6 %copy-start.4 = (bf16[256,512]{1,0:T(8,128)(2,1)S(1)}, bf16[256,512]{1,0:T(8,128)(2,1)}, u32[]{:S(2)}) copy-start(bf16[256,512]{1,0:T(8,128)(2,1)} %param.10) | copy-start | bytes 786436
  1.2 0.7 copy-start.6
  1.8 0.7 copy-start.7
  2.5 0.7 copy-start.5
  3.2 1.2 %copy-start = (bf16[256,2048]{1,0:T(8,128)(2,1)S(1)}, bf16[256,2048]{1,0:T(8,128)(2,1)}, u32[]{:S(2)}) copy-start(bf16[256,2048]{1,0:T(8,128)(2,1)} %dz_hbm.1) | copy-start | bytes 3145732
  4.4 1.2 %copy-start.1 = (bf16[256,2048]{1,0:T(8,128)(2,1)S(1)}, bf16[256,2048]{1,0:T(8,128)(2,1)}, u32[]{:S(2)}) copy-start(bf16[256,2048]{1,0:T(8,128)(2,1)} %dr_hbm.1) | copy-start | bytes 3145732
  5.6 1.2 %copy-start.2 = (bf16[256,2048]{1,0:T(8,128)(2,1)S(1)}, bf16[256,2048]{1,0:T(8,128)(2,1)}, u32[]{:S(2)}) copy-start(bf16[256,2048]{1,0:T(8,128)(2,1)} %dl_hbm.1) | copy-start | bytes 3145732
  6.9 1.0 copy-start.3

commit v2 on v1

--- a/solution.py
+++ b/solution.py
@@ -15,39 +15,61 @@
 
 
 def kernel(
-    head_ref, src_ref, live_ref, coup_ref, rot_ref, low_ref, up_ref, dz_hbm, dr_hbm, dl_hbm,
+    head_ref, src_ref, live_ref, coup_ref, rot_ref, low_hbm, up_hbm, dz_hbm, dr_hbm, dl_hbm,
     out_ref,
-    send_buf, recv_buf, sta, stb, stc, std_, ua, ub, uc, ud, stage_low, low_all, dip, half, amp, parts,
-    dip_sem, a_send, a_recv, q_send, q_recv, g_send, g_recv, l_send, l_recv, m_send, m_recv, r_send, r_recv,
+    low_ref, up_ref, up_send, up_mid, up_recv, low_send, low_mid, low_recv,
+    sta, stb, stc, std_, ua, ub, uc, ud, stage_low, low_all, dip, half, amp, part1, row_sum, part2,
+    ready, in_sem, dip_sem, s1, r1, s2, r2, q_send, q_recv, g_send, g_recv, l_send, l_recv, m_send, m_recv,
 ):
     ka = lax.axis_index("ka")
     vert = lax.axis_index("vert")
-    me = ka * 32 + vert
     yy = vert // 8
     xx = (vert // 4) % 2
     zz = vert % 4
+    row = ka * 2 + xx
+    plane = yy * 4 + zz
     stages = (sta, stb, stc, std_)
     uppers = (ua, ub, uc, ud)
 
+    def in_row(p):
+        return p // 2, yy * 8 + (p % 2) * 4 + zz
+
+    def in_plane(w):
+        return ka, (w // 4) * 8 + xx * 4 + w % 4
+
+    def say(sem, to):
+        pl.semaphore_signal(sem, inc=1, device_id=to, device_id_type=MESH)
+
+    def take(ref, sem):
+        pltpu.make_async_copy(ref, ref, sem).wait()
+
+    def send(src, dst, out_sem, in_sem_, to):
+        copy = pltpu.make_async_remote_copy(
+            src_ref=src, dst_ref=dst, send_sem=out_sem, recv_sem=in_sem_, device_id=to, device_id_type=MESH
+        )
+        copy.start()
+        return copy
+
     barrier = pltpu.get_barrier_semaphore()
-
-    def greet(k, _):
-        pl.semaphore_signal(
-            barrier, inc=1, device_id=((ka + k // 32) % 4, (vert + k % 32) % 32), device_id_type=MESH
-        )
-        return 0
-
-    lax.fori_loop(1, 128, greet, 0)
+    for k in range(1, 8):
+        say(barrier, in_row((row + k) % 8))
+    for k in range(1, 4):
+        say(barrier, in_plane(((yy + k) % 4) * 4 + zz))
+        say(barrier, in_plane(yy * 4 + (zz + k) % 4))
+    loads = [pltpu.make_async_copy(h, v, in_sem.at[n]) for n, (h, v) in enumerate(((up_hbm, up_ref), (low_hbm, low_ref)))]
     dips = [pltpu.make_async_copy(h, dip.at[n], dip_sem.at[n]) for n, h in enumerate((dz_hbm, dr_hbm, dl_hbm))]
-    for c in dips:
+    for c in loads + dips:
         c.start()
+    for c in loads:
+        c.wait()
 
     lane = lax.broadcasted_iota(jnp.int32, (8, 128), 1)
     zeros = jnp.zeros((8, 128), jnp.int32)
-    heads = [zeros + head_ref[me * 4 + r] for r in range(4)]
+    heads = [zeros + head_ref[(ka * 32 + vert) * 4 + r] for r in range(4)]
     owned = [[(heads[r] >= o * 128) & (heads[r] < (o + 1) * 128) for r in range(3)] for o in range(4)]
 
     def pack(j, _):
+        x2, w2 = (j // 4) % 2, (j // 8) * 4 + j % 4
         for u in range(3):
             unit = up_ref[j] if u == 0 else low_ref[2 * j + u - 1]
             runs = [unit[:, r * 128:(r + 1) * 128].astype(F32) for r in range(4)]
@@ -55,23 +77,32 @@
                 value = runs[3]
                 for r in range(3):
                     value = jnp.where(owned[o][r], runs[r], value)
-                send_buf[o * 32 + j, u] = value.astype(BF16)
+                if u == 0:
+                    up_send[o * 2 + x2, w2] = value.astype(BF16)
+                else:
+                    low_send[w2, o * 2 + x2, u - 1] = value.astype(BF16)
         return 0
 
     lax.fori_loop(0, 32, pack, 0)
-    pl.semaphore_wait(barrier, 127)
-
-    def spread(k, _):
-        ka2, v2 = (ka + k // 32) % 4, (vert + k % 32) % 32
-        pltpu.make_async_remote_copy(
-            src_ref=send_buf.at[ka2 * 32 + v2], dst_ref=recv_buf.at[me],
-            send_sem=a_send, recv_sem=a_recv, device_id=(ka2, v2), device_id_type=MESH,
-        ).start()
-        return 0
-
-    lax.fori_loop(1, 128, spread, 0)
-    recv_buf[me] = send_buf[me]
-    pltpu.make_async_copy(recv_buf.at[pl.ds(0, 127)], recv_buf.at[pl.ds(0, 127)], a_recv).wait()
+    pl.semaphore_wait(barrier, 13)
+
+    for k in range(1, 8):
+        p = (row + k) % 8
+        send(up_send.at[p], up_mid.at[row], s1.at[0], r1.at[0], in_row(p))
+    for k in range(1, 4):
+        say(ready, in_plane(yy * 4 + (zz + k) % 4))
+    up_mid[row] = up_send[row]
+    pl.semaphore_wait(ready, 3)
+    take(up_mid.at[pl.ds(0, 7)], r1.at[0])
+    for k in range(1, 16):
+        w = (plane + k) % 16
+        send(up_mid.at[:, w], up_recv.at[plane], s2.at[0], r2.at[0], in_plane(w))
+    up_recv[plane] = up_mid[:, plane]
+    for k in range(1, 16):
+        w = (plane + k) % 16
+        send(low_send.at[w], low_mid.at[plane], s1.at[1], r1.at[1], in_plane(w))
+    low_mid[plane] = low_send[plane]
+    take(up_recv.at[pl.ds(0, 15)], r2.at[0])
 
     lives = [live_ref[2 * ka + b] for b in range(2)]
 
@@ -81,7 +112,7 @@
             halves = []
             for b in range(2):
                 s = src_ref[ka * 128 + b * 64 + block]
-                tile = recv_buf[s, 0].astype(F32)
+                tile = up_recv[s // 8, s % 8].astype(F32)
                 halves.append(jnp.where(lane + block * 128 < lives[b], tile, 0.0))
             both = jnp.concatenate(halves, axis=0).astype(BF16)
             for c in range(4):
@@ -94,18 +125,20 @@
 
     exchanges = []
     for c in range(4):
-        row = []
+        copies = []
         for d in range(1, 4):
             q = (ka + d) % 4
-            copy = pltpu.make_async_remote_copy(
-                src_ref=stages[c].at[q], dst_ref=uppers[c].at[yy, xx, zz, ka],
-                send_sem=q_send.at[c, d - 1], recv_sem=q_recv.at[c, d - 1],
-                device_id=(q, vert), device_id_type=MESH,
-            )
-            copy.start()
-            row.append(copy)
-        exchanges.append(row)
+            copies.append(send(
+                stages[c].at[q], uppers[c].at[yy, xx, zz, ka], q_send.at[c, d - 1], q_recv.at[c, d - 1], (q, vert)
+            ))
+        exchanges.append(copies)
         uppers[c][yy, xx, zz, ka] = stages[c][ka]
+
+    take(low_mid.at[pl.ds(0, 15)], r1.at[1])
+    for k in range(1, 8):
+        p = (row + k) % 8
+        send(low_mid.at[:, p], low_recv.at[:, row], s2.at[1], r2.at[1], in_row(p))
+    low_recv[:, row] = low_mid[:, row]
 
     def arrange_low(v, _):
         for b in range(2):
@@ -114,24 +147,16 @@
                 s = src_ref[ka * 128 + b * 64 + block]
                 keep = lane + block * 128 < lives[b]
                 both = jnp.concatenate(
-                    [jnp.where(keep, recv_buf[s, u].astype(F32), 0.0) for u in (1, 2)], axis=0
+                    [jnp.where(keep, low_recv[s // 8, s % 8, u].astype(F32), 0.0) for u in range(2)], axis=0
                 ).astype(BF16)
                 at = b * 256 + h * 128
                 stage_low[v, :, at:at + 128] = both
         return 0
 
-    lax.fori_loop(0, 32, arrange_low, 0)
-
     def spread_low(k, _):
         v2 = (vert + k) % 32
-        pltpu.make_async_remote_copy(
-            src_ref=stage_low.at[v2], dst_ref=low_all.at[ka, vert],
-            send_sem=l_send, recv_sem=l_recv, device_id=(ka, v2), device_id_type=MESH,
-        ).start()
+        send(stage_low.at[v2], low_all.at[ka, vert], l_send, l_recv, (ka, v2))
         return 0
-
-    lax.fori_loop(1, 32, spread_low, 0)
-    low_all[ka, vert] = stage_low[vert]
 
     def vid(y, x, z):
         return y * 8 + x * 4 + z
@@ -218,7 +243,13 @@
         next(chains[c])
     for c in (2, 3, 0, 1):
         next(chains[c])
-    pltpu.make_async_copy(low_all.at[0, pl.ds(0, 31)], low_all.at[0, pl.ds(0, 31)], l_recv).wait()
+    take(low_recv.at[:, pl.ds(0, 7)], r2.at[1])
+    lax.fori_loop(0, 32, arrange_low, 0)
+    lax.fori_loop(1, 32, spread_low, 0)
+    low_all[ka, vert] = stage_low[vert]
+    for c in (2, 3, 0, 1):
+        next(chains[c])
+    take(low_all.at[0, pl.ds(0, 31)], l_recv)
     moves.append(low_copy(0, ka, sibling))
     moves.append(low_copy(1, ka, across))
     for m in moves:
@@ -241,7 +272,7 @@
         c.wait()
 
     def factor(k, d):
-        return rot_ref[k, d] * coup_ref[k, d].astype(F32)
+        return rot_ref[d, k] * coup_ref[d, k].astype(F32)
 
     def step(g, _):
         y, x = g // 2, g % 2
@@ -274,30 +305,36 @@
             lows = low_all[o, pl.ds(t * 8, 8)].reshape(128, 512)
             term = lax.dot_general(half[:, o * 512:(o + 1) * 512], lows, NT, preferred_element_type=F32)
             total = term if total is None else total + term
-        amp[t] = total.reshape(32, 8, 128)
-
-    def give(k, _):
-        ka2, v2 = (ka + k // 32) % 4, (vert + k % 32) % 32
-        pltpu.make_async_remote_copy(
-            src_ref=amp.at[ka2, v2], dst_ref=parts.at[me],
-            send_sem=r_send, recv_sem=r_recv, device_id=(ka2, v2), device_id_type=MESH,
-        ).start()
-        return 0
-
-    lax.fori_loop(1, 128, give, 0)
-    parts[me] = amp[ka, vert]
-    pltpu.make_async_copy(parts.at[pl.ds(0, 127)], parts.at[pl.ds(0, 127)], r_recv).wait()
-    total = jnp.sum(parts[...], axis=0)
+        tiles = total.reshape(32, 8, 128)
+        for j in range(32):
+            amp[(j // 8) * 4 + j % 4, t * 2 + (j // 4) % 2] = tiles[j]
+
+    for k in range(1, 16):
+        w = (plane + k) % 16
+        send(amp.at[w], part1.at[plane], s1.at[2], r1.at[2], in_plane(w))
+    part1[plane] = amp[plane]
+    take(part1.at[pl.ds(0, 15)], r1.at[2])
+    row_sum[...] = jnp.sum(part1[...], axis=0)
+    for k in range(1, 8):
+        p = (row + k) % 8
+        send(row_sum.at[p], part2.at[row], s2.at[2], r2.at[2], in_row(p))
+    part2[row] = row_sum[row]
+    take(part2.at[pl.ds(0, 7)], r2.at[2])
+    total = jnp.sum(part2[...], axis=0)
     out_ref[...] = total * total
 
-    pltpu.make_async_copy(send_buf.at[pl.ds(0, 127)], send_buf.at[pl.ds(0, 127)], a_send).wait()
-    for row in exchanges:
-        for copy in row:
+    take(up_send.at[pl.ds(0, 7)], s1.at[0])
+    take(up_recv.at[pl.ds(0, 15)], s2.at[0])
+    take(low_send.at[pl.ds(0, 15)], s1.at[1])
+    take(low_recv.at[:, pl.ds(0, 7)], s2.at[1])
+    for copies in exchanges:
+        for copy in copies:
             copy.wait_send()
-    pltpu.make_async_copy(stage_low.at[pl.ds(0, 31)], stage_low.at[pl.ds(0, 31)], l_send).wait()
+    take(stage_low.at[pl.ds(0, 31)], l_send)
     for copy in sent + moves:
         copy.wait_send()
-    pltpu.make_async_copy(parts.at[pl.ds(0, 127)], parts.at[pl.ds(0, 127)], r_send).wait()
+    take(amp.at[pl.ds(0, 15)], s1.at[2])
+    take(row_sum.at[pl.ds(0, 7)], s2.at[2])
 
 
 def per_device(
@@ -305,7 +342,9 @@
 ):
     heads = layout_map.reshape(512, 128)[:, 0] // 128
     hits = heads[None, :] == jnp.arange(512, dtype=jnp.int32)[:, None]
-    source = jnp.sum(jnp.where(hits, (jnp.arange(512, dtype=jnp.int32) // 4)[None, :], 0), axis=1)
+    device = jnp.arange(512, dtype=jnp.int32) // 4
+    place = ((device // 8) % 4 * 4 + device % 4) * 8 + device // 32 * 2 + device // 4 % 2
+    source = jnp.sum(jnp.where(hits, place[None, :], 0), axis=1)
     smem = pl.BlockSpec(memory_space=pltpu.SMEM)
     vmem = pl.BlockSpec(memory_space=pltpu.VMEM)
     hbm = pl.BlockSpec(memory_space=pl.ANY)
@@ -313,33 +352,41 @@
     out = pl.pallas_call(
         kernel,
         out_shape=jax.ShapeDtypeStruct((8, 128), F32),
-        in_specs=[smem] * 5 + [vmem] * 2 + [hbm] * 3,
+        in_specs=[smem] * 5 + [hbm] * 5,
         out_specs=vmem,
         scratch_shapes=[
-            pltpu.VMEM((128, 3, 8, 128), BF16),
-            pltpu.VMEM((128, 3, 8, 128), BF16),
+            pltpu.VMEM((64, 8, 512), BF16),
+            pltpu.VMEM((32, 8, 512), BF16),
+            pltpu.VMEM((8, 16, 8, 128), BF16),
+            pltpu.VMEM((8, 16, 8, 128), BF16),
+            pltpu.VMEM((16, 8, 8, 128), BF16),
+            pltpu.VMEM((16, 8, 2, 8, 128), BF16),
+            pltpu.VMEM((16, 8, 2, 8, 128), BF16),
+            pltpu.VMEM((16, 8, 2, 8, 128), BF16),
             *[pltpu.VMEM((4, 16, w), BF16) for w in WIDTHS],
             *[pltpu.VMEM((4, 2, 4, 4, 16, w), BF16) for w in WIDTHS],
             pltpu.VMEM((32, 16, 512), BF16),
             pltpu.VMEM((4, 32, 16, 512), BF16),
             pltpu.VMEM((3, 256, 2048), BF16),
             pltpu.VMEM((256, 2048), BF16),
-            pltpu.VMEM((4, 32, 8, 128), F32),
-            pltpu.VMEM((128, 8, 128), F32),
-            dma((3,)),
-            dma, dma,
+            pltpu.VMEM((16, 8, 8, 128), F32),
+            pltpu.VMEM((16, 8, 8, 128), F32),
+            pltpu.VMEM((8, 8, 128), F32),
+            pltpu.VMEM((8, 8, 128), F32),
+            pltpu.SemaphoreType.REGULAR,
+            dma((2,)), dma((3,)),
+            dma((3,)), dma((3,)), dma((3,)), dma((3,)),
             dma((4, 3)), dma((4, 3)),
             dma((4, 9)), dma((4, 9)),
             dma, dma,
             dma((3,)), dma((3,)),
-            dma, dma,
         ],
         compiler_params=pltpu.CompilerParams(
-            collective_id=0, has_side_effects=True, vmem_limit_bytes=48 * 1024 * 1024
+            collective_id=0, has_side_effects=True, vmem_limit_bytes=60 * 1024 * 1024
         ),
         cost_estimate=pl.CostEstimate(flops=7_000_000_000, bytes_accessed=5_000_000, transcendentals=0),
     )(
-        heads, source, block_live, coupling, rot_coef,
+        heads, source, block_live, coupling.T, rot_coef.T,
         eig_lower.reshape(64, 8, 512), eig_upper.reshape(32, 8, 512), dip_zero, dip_raise, dip_lower,
     )
     return out.T

time: 110 us -> 109 us (level)
  local copies, waits for them, and re-layouts: 8.27 us -> 2.37 us
  Pallas kernels: 101 us -> 106 us
    unnamed x19 -> x3, local copies, waits for them, and re-layouts: 7.14 us -> 1.28 us
    pallas_call x1, Pallas kernels: 101 us -> 106 us  [per_device(): pl.pallas_call(kernel, out_shape=jax.ShapeDtypeStruct((8, 128), F32), in_...]
where the time goes in v2:
time: 109 us
  Pallas kernels  106 us (97%)
  local copies, waits for them, and re-layouts  2.37 us (2%)
    pallas_call x1, Pallas kernels, per_device(): pl.pallas_call(kernel, out_shape=jax.ShapeDtypeStruct((8, 128), F32), in_...  106 us

profile of v2, /device:TPU:1, one launch (start us, length us, event | category | flops | bytes accessed | tf_op | source)
XLA Modules:
  0.0 109.2 jit_solution(12866095191816353730)
XLA Ops:
  0.0 1.1 slice_reduce_fusion
  1.1 0.0 copy-start
  1.1 0.8 select_reduce_fusion.src_ref
  1.9 0.0 copy-done
  1.9 106.0 %shard_map.91 = f32[8,128]{1,0:T(8,128)} custom-call(s32[512]{0:T(512)} %copy-done, s32[512]{0:T(512)} %select_reduce_fusion.src_ref, s32[8]{0:T(128)} %live_ref.1, s32[3,8]{1,0:T(4,128)} %bitcast.10, f32[3,8]{1,0:T(4,128)} %bitcast.11, bf16[64,8,512]{2,1,0:T(8,128)(2,1)} %bitcast.8, bf16[32,8,512]{2,1,0:T(8,128)(2,1)} %bitcast.9, bf16[256,2048]{1,0:T(8,128)(2,1)} %dz_hbm.1, ...), custom_call_target="tpu_custom_call" | custom-call | flops 7000000000 | bytes 5000000 | tf_op jit(solution)/shard_map/pallas_call | solution.py:352
  107.9 1.3 %copy.11 = f32[128,8]{0,1:T(8,128)} copy(f32[128,8]{0,1:T(8,128)} %bitcast.7) | data formatting | bytes 8192
  (1 shorter events, 0.0 us)
Async XLA Ops:
  1.1 0.8 copy-start

commit v3 on v2

--- a/solution.py
+++ b/solution.py
@@ -18,7 +18,7 @@
     head_ref, src_ref, live_ref, coup_ref, rot_ref, low_hbm, up_hbm, dz_hbm, dr_hbm, dl_hbm,
     out_ref,
     low_ref, up_ref, up_send, up_mid, up_recv, low_send, low_mid, low_recv,
-    sta, stb, stc, std_, ua, ub, uc, ud, stage_low, low_all, dip, half, amp, part1, row_sum, part2,
+    sta, stb, stc, std_, ua, ub, uc, ud, stage_low, low_all, dip, acc, half, amp, pair, part,
     ready, in_sem, dip_sem, s1, r1, s2, r2, q_send, q_recv, g_send, g_recv, l_send, l_recv, m_send, m_recv,
 ):
     ka = lax.axis_index("ka")
@@ -84,6 +84,13 @@
         return 0
 
     lax.fori_loop(0, 32, pack, 0)
+
+    def clear(y, _):
+        for n in range(3):
+            acc[n, y] = jnp.zeros((2, 4, 64, 256), F32)
+        return 0
+
+    lax.fori_loop(0, 4, clear, 0)
     pl.semaphore_wait(barrier, 13)
 
     for k in range(1, 8):
@@ -93,14 +100,14 @@
         say(ready, in_plane(yy * 4 + (zz + k) % 4))
     up_mid[row] = up_send[row]
     pl.semaphore_wait(ready, 3)
+    for k in range(1, 16):
+        w = (plane + k) % 16
+        send(low_send.at[w], low_mid.at[plane], s1.at[1], r1.at[1], in_plane(w))
     take(up_mid.at[pl.ds(0, 7)], r1.at[0])
     for k in range(1, 16):
         w = (plane + k) % 16
         send(up_mid.at[:, w], up_recv.at[plane], s2.at[0], r2.at[0], in_plane(w))
     up_recv[plane] = up_mid[:, plane]
-    for k in range(1, 16):
-        w = (plane + k) % 16
-        send(low_send.at[w], low_mid.at[plane], s1.at[1], r1.at[1], in_plane(w))
     low_mid[plane] = low_send[plane]
     take(up_recv.at[pl.ds(0, 15)], r2.at[0])
 
@@ -134,12 +141,6 @@
         exchanges.append(copies)
         uppers[c][yy, xx, zz, ka] = stages[c][ka]
 
-    take(low_mid.at[pl.ds(0, 15)], r1.at[1])
-    for k in range(1, 8):
-        p = (row + k) % 8
-        send(low_mid.at[:, p], low_recv.at[:, row], s2.at[1], r2.at[1], in_row(p))
-    low_recv[:, row] = low_mid[:, row]
-
     def arrange_low(v, _):
         for b in range(2):
             for h in range(2):
@@ -163,70 +164,102 @@
 
     sent = []
 
+    where = {"y": yy, "x": xx, "z": zz}
+    sizes = {"y": 4, "x": 2, "z": 4}
+
     def chain(c):
         u = uppers[c]
-        where = {"y": yy, "x": xx, "z": zz}
-        have = {"y": False, "x": False, "z": False}
+        first, second, last = ORDERS[c]
+        done = []
         count = 0
 
-        def region(fixed):
+        def region(fixed, have):
             idx = []
-            for name, size in (("y", 4), ("x", 2), ("z", 4)):
+            for name in "yxz":
                 if name in fixed:
                     idx.append(fixed[name])
-                elif have[name]:
-                    idx.append(pl.ds(0, size))
+                elif name in have:
+                    idx.append(pl.ds(0, sizes[name]))
                 else:
                     idx.append(where[name])
             return u.at[tuple(idx)]
 
         def go(ref, axis, step):
             nonlocal count
-            size = 2 if axis == "x" else 4
             to = dict(where)
-            to[axis] = (where[axis] + step) % size
-            copy = pltpu.make_async_remote_copy(
-                src_ref=ref, dst_ref=ref, send_sem=g_send.at[c, count], recv_sem=g_recv.at[c, count],
-                device_id=(ka, vid(to["y"], to["x"], to["z"])), device_id_type=MESH,
+            to[axis] = (where[axis] + step) % sizes[axis]
+            copy = send(
+                ref, ref, g_send.at[c, count], g_recv.at[c, count], (ka, vid(to["y"], to["x"], to["z"]))
             )
             count += 1
-            copy.start()
             sent.append(copy)
             return copy
 
-        for axis in ORDERS[c]:
-            here = where[axis]
+        def both(axis, fixed, have):
+            ref = region(fixed, have)
             if axis == "x":
-                one = go(region({"x": here}), "x", 1)
-                yield
-                one.wait_recv()
-            else:
-                plus = go(region({axis: here}), axis, 1)
-                minus = go(region({axis: here}), axis, 3)
-                yield
-                before, after = (here + 3) % 4, (here + 1) % 4
-                other = "z" if axis == "y" else "y"
-                if have[other]:
-                    first, second = {other: pl.ds(0, 2)}, {other: pl.ds(2, 2)}
-                    cut = None
-                elif have["x"]:
-                    first, second = {"x": 0}, {"x": 1}
-                    cut = None
-                else:
-                    first, second = {}, {}
-                    cut = True
-                plus.wait_recv()
-                r1 = region({axis: before, **first})
-                on1 = go(r1.at[pl.ds(0, 2)] if cut else r1, axis, 1)
-                minus.wait_recv()
-                r2 = region({axis: after, **second})
-                on2 = go(r2.at[pl.ds(2, 2)] if cut else r2, axis, 3)
-                yield
-                on1.wait_recv()
-                on2.wait_recv()
-            have[axis] = True
+                return [go(ref, axis, 1)]
+            return [go(ref, axis, 1), go(ref, axis, 3)]
+
+        def onward(pair, axis, fixed, have, cut):
+            before, after = (where[axis] + 3) % 4, (where[axis] + 1) % 4
+            halves = ({}, {})
+            if cut == "x":
+                halves = ({"x": 0}, {"x": 1})
+            elif cut in ("y", "z"):
+                halves = ({cut: pl.ds(0, 2)}, {cut: pl.ds(2, 2)})
+            out = []
+            for side, (copy, came, step) in enumerate(((pair[0], before, 1), (pair[1], after, 3))):
+                copy.wait_recv()
+                ref = region({**fixed, axis: came, **halves[side]}, have)
+                if cut == "o":
+                    ref = ref.at[pl.ds(2 * side, 2)]
+                out.append(go(ref, axis, step))
+            return out
+
+        begun = both(first, {}, "")
+        yield
+        if first == "x":
+            begun[0].wait_recv()
+        else:
+            on = onward(begun, first, {}, "", "o")
+            yield
+            for copy in on:
+                copy.wait_recv()
+        cut = first
+        here = where[second]
+        middle = both(second, {}, first)
+        batches = [({second: here}, both(last, {}, first))]
+        yield
+        on = onward(middle, second, {}, first, cut)
+        for step in (3, 1):
+            at = {second: (here + step) % 4}
+            batches.append((at, both(last, at, first)))
+        yield
+        for copy in on:
+            copy.wait_recv()
+        at = {second: (here + 2) % 4}
+        batches.append((at, both(last, at, first)))
+        yield
+        if last == "x":
+            for _, copies in batches:
+                copies[0].wait_recv()
+            yield
+            return
+        ends = []
+        for group in (batches[:1], batches[1:3], batches[3:]):
+            for at, copies in group:
+                ends.extend(onward(copies, last, at, first, "x"))
+            yield
+        for copy in ends:
+            copy.wait_recv()
+        yield
 
     chains = [chain(c) for c in range(4)]
+
+    def run(*names):
+        for c in names:
+            next(chains[c])
 
     def low_copy(slot, owner, to):
         return pltpu.make_async_remote_copy(
@@ -237,55 +270,92 @@
     sibling = (ka // 2) * 2 + (ka + 1) % 2
     across = (ka + 2) % 4
     moves = []
-    for c in range(4):
+    def term(c, n, rows):
+        flat = rows.reshape(-1, WIDTHS[c])
+        value = lax.dot_general(
+            flat, dip[n, :, STARTS[c]:STARTS[c] + WIDTHS[c]], NT, preferred_element_type=F32
+        )
+        return value
+
+    def add_z(z):
+        def body(n, _):
+            acc[n, :, :, z] += term(0, n, ua[:, :, z]).reshape(4, 2, 64, 256)
+            return 0
+
+        lax.fori_loop(0, 3, body, 0)
+
+    def add_y(y):
+        def body(n, _):
+            acc[n, y] += term(1, n, ub[y]).reshape(2, 4, 64, 256)
+            return 0
+
+        lax.fori_loop(0, 3, body, 0)
+
+    def add_x(x):
+        def body(n, _):
+            acc[n, :, x] += (term(2, n, uc[:, x]) + term(3, n, ud[:, x])).reshape(4, 4, 64, 256)
+            return 0
+
+        lax.fori_loop(0, 3, body, 0)
+
+    for c in (2, 3, 0, 1):
         for copy in exchanges[c]:
             copy.wait_recv()
-        next(chains[c])
-    for c in (2, 3, 0, 1):
-        next(chains[c])
+        run(c)
+    run(2, 3)
+    run(0, 1)
+    take(low_mid.at[pl.ds(0, 15)], r1.at[1])
+    for k in range(1, 8):
+        p = (row + k) % 8
+        send(low_mid.at[:, p], low_recv.at[:, row], s2.at[1], r2.at[1], in_row(p))
+    low_recv[:, row] = low_mid[:, row]
+    run(2, 3)
+    run(0, 1)
     take(low_recv.at[:, pl.ds(0, 7)], r2.at[1])
     lax.fori_loop(0, 32, arrange_low, 0)
     lax.fori_loop(1, 32, spread_low, 0)
     low_all[ka, vert] = stage_low[vert]
-    for c in (2, 3, 0, 1):
-        next(chains[c])
+    run(2, 3)
+    run(0, 1)
+    run(0, 1)
+    run(2, 3)
+    for c in dips:
+        c.wait()
     take(low_all.at[0, pl.ds(0, 31)], l_recv)
     moves.append(low_copy(0, ka, sibling))
     moves.append(low_copy(1, ka, across))
     for m in moves:
         m.start()
-    for c in (2, 3, 0, 1):
-        next(chains[c])
-    for c in (2, 3, 0, 1):
-        next(chains[c])
+    run(0, 1)
+    add_z(zz)
+    add_y(yy)
+    run(0, 1)
+
+    def sides(k, _):
+        add_z((zz + 3 - 2 * k) % 4)
+        add_y((yy + 3 - 2 * k) % 4)
+        return 0
+
+    lax.fori_loop(0, 2, sides, 0)
+    add_x(xx)
     moves[1].wait_recv()
     moves.append(low_copy(2, across, sibling))
     moves[2].start()
-    live_chains = [2, 3, 0, 1]
-    while live_chains:
-        for c in list(live_chains):
-            if next(chains[c], "end") == "end":
-                live_chains.remove(c)
+    run(2, 3)
+    add_x(1 - xx)
+    run(0)
+    add_z((zz + 2) % 4)
+    run(1)
+    add_y((yy + 2) % 4)
     moves[0].wait_recv()
     moves[2].wait_recv()
-    for c in dips:
-        c.wait()
 
     def factor(k, d):
         return rot_ref[d, k] * coup_ref[d, k].astype(F32)
 
     def step(g, _):
         y, x = g // 2, g % 2
-        sums = []
-        for n in range(3):
-            total = None
-            for c in range(4):
-                rows = uppers[c][y, x].reshape(256, WIDTHS[c])
-                term = lax.dot_general(
-                    rows, dip[n, :, STARTS[c]:STARTS[c] + WIDTHS[c]], NT, preferred_element_type=F32
-                )
-                total = term if total is None else total + term
-            sums.append(total.reshape(4, 8, 8, 256))
+        sums = [acc[n, y, x].reshape(4, 8, 8, 256) for n in range(3)]
         zero, up, down = sums
         rows = pl.ds(pl.multiple_of(g * 32, 32), 32)
         for k in range(8):
@@ -306,21 +376,23 @@
             term = lax.dot_general(half[:, o * 512:(o + 1) * 512], lows, NT, preferred_element_type=F32)
             total = term if total is None else total + term
         tiles = total.reshape(32, 8, 128)
-        for j in range(32):
-            amp[(j // 8) * 4 + j % 4, t * 2 + (j // 4) % 2] = tiles[j]
-
-    for k in range(1, 16):
-        w = (plane + k) % 16
-        send(amp.at[w], part1.at[plane], s1.at[2], r1.at[2], in_plane(w))
-    part1[plane] = amp[plane]
-    take(part1.at[pl.ds(0, 15)], r1.at[2])
-    row_sum[...] = jnp.sum(part1[...], axis=0)
-    for k in range(1, 8):
-        p = (row + k) % 8
-        send(row_sum.at[p], part2.at[row], s2.at[2], r2.at[2], in_row(p))
-    part2[row] = row_sum[row]
-    take(part2.at[pl.ds(0, 7)], r2.at[2])
-    total = jnp.sum(part2[...], axis=0)
+        amp[t % 2, t // 2] = tiles
+
+    core, side = ka % 2, ka // 2
+    to_pair = send(amp.at[1 - core], pair, s1.at[2], r1.at[2], (sibling, vert))
+    to_pair.wait_recv()
+    pair[...] = pair[...] + amp[core]
+    mine = side * 32 + vert
+
+    def give(k, _):
+        h2, v2 = (side + k // 32) % 2, (vert + k % 32) % 32
+        send(pair.at[h2, v2], part.at[mine], s2.at[2], r2.at[2], (h2 * 2 + core, v2))
+        return 0
+
+    lax.fori_loop(1, 64, give, 0)
+    part[mine] = pair[side, vert]
+    take(part.at[pl.ds(0, 63)], r2.at[2])
+    total = jnp.sum(part[...], axis=0)
     out_ref[...] = total * total
 
     take(up_send.at[pl.ds(0, 7)], s1.at[0])
@@ -333,8 +405,8 @@
     take(stage_low.at[pl.ds(0, 31)], l_send)
     for copy in sent + moves:
         copy.wait_send()
-    take(amp.at[pl.ds(0, 15)], s1.at[2])
-    take(row_sum.at[pl.ds(0, 7)], s2.at[2])
+    to_pair.wait_send()
+    take(part.at[pl.ds(0, 63)], s2.at[2])
 
 
 def per_device(
@@ -368,16 +440,16 @@
             pltpu.VMEM((32, 16, 512), BF16),
             pltpu.VMEM((4, 32, 16, 512), BF16),
             pltpu.VMEM((3, 256, 2048), BF16),
+            pltpu.VMEM((3, 4, 2, 4, 64, 256), F32),
             pltpu.VMEM((256, 2048), BF16),
-            pltpu.VMEM((16, 8, 8, 128), F32),
-            pltpu.VMEM((16, 8, 8, 128), F32),
-            pltpu.VMEM((8, 8, 128), F32),
-            pltpu.VMEM((8, 8, 128), F32),
+            pltpu.VMEM((2, 2, 32, 8, 128), F32),
+            pltpu.VMEM((2, 32, 8, 128), F32),
+            pltpu.VMEM((64, 8, 128), F32),
             pltpu.SemaphoreType.REGULAR,
             dma((2,)), dma((3,)),
             dma((3,)), dma((3,)), dma((3,)), dma((3,)),
             dma((4, 3)), dma((4, 3)),
-            dma((4, 9)), dma((4, 9)),
+            dma((4, 24)), dma((4, 24)),
             dma, dma,
             dma((3,)), dma((3,)),
         ],

time: 109 us -> 102 us (0.936)
  Pallas kernels: 106 us -> 99.1 us
    pallas_call x1, Pallas kernels: 106 us -> 99.1 us  [per_device(): pl.pallas_call(kernel, out_shape=jax.ShapeDtypeStruct((8, 128), F32), in_...]
where the time goes in v3:
time: 102 us
  Pallas kernels  99.1 us (97%)
  local copies, waits for them, and re-layouts  2.37 us (2%)
    pallas_call x1, Pallas kernels, per_device(): pl.pallas_call(kernel, out_shape=jax.ShapeDtypeStruct((8, 128), F32), in_...  99.1 us

profile of v3, /device:TPU:1, one launch (start us, length us, event | category | flops | bytes accessed | tf_op | source)
XLA Modules:
  0.0 102.3 jit_solution(10587470679690028423)
XLA Ops:
  0.0 1.1 %slice_reduce_fusion = s32[512]{0:T(512)S(1)} fusion(s32[512,128]{1,0:T(8,128)} %bitcast.6), kind=kLoop, calls=%fused_computation.2 | loop fusion | bytes 4096 | tf_op jit(solution)/shard_map/slice | solution.py:415
  1.1 0.0 copy-start
  1.1 0.8 select_reduce_fusion.src_ref
  1.9 0.0 copy-done
  1.9 99.1 %shard_map.91 = f32[8,128]{1,0:T(8,128)} custom-call(s32[512]{0:T(512)} %copy-done, s32[512]{0:T(512)} %select_reduce_fusion.src_ref, s32[8]{0:T(128)} %live_ref.1, s32[3,8]{1,0:T(4,128)} %bitcast.10, f32[3,8]{1,0:T(4,128)} %bitcast.11, bf16[64,8,512]{2,1,0:T(8,128)(2,1)} %bitcast.8, bf16[32,8,512]{2,1,0:T(8,128)(2,1)} %bitcast.9, bf16[256,2048]{1,0:T(8,128)(2,1)} %dz_hbm.1, ...), custom_call_target="tpu_custom_call" | custom-call | flops 7000000000 | bytes 5000000 | tf_op jit(solution)/shard_map/pallas_call | solution.py:424
  101.0 1.3 %copy.11 = f32[128,8]{0,1:T(8,128)} copy(f32[128,8]{0,1:T(8,128)} %bitcast.7) | data formatting | bytes 8192
  (1 shorter events, 0.0 us)
Async XLA Ops:
  1.1 0.8 copy-start

commit v4 on v3

--- a/solution.py
+++ b/solution.py
@@ -17,8 +17,8 @@
 def kernel(
     head_ref, src_ref, live_ref, coup_ref, rot_ref, low_hbm, up_hbm, dz_hbm, dr_hbm, dl_hbm,
     out_ref,
-    low_ref, up_ref, up_send, up_mid, up_recv, low_send, low_mid, low_recv,
-    sta, stb, stc, std_, ua, ub, uc, ud, stage_low, low_all, dip, acc, half, amp, pair, part,
+    low_ref, up_ref, up_send, up_recv, low_send, low_mid, low_recv,
+    sta, stb, stc, std_, ua, ub, uc, ud, stage_low, low_plane, low_all, dip, acc, half, amp, pair, part,
     ready, in_sem, dip_sem, s1, r1, s2, r2, q_send, q_recv, g_send, g_recv, l_send, l_recv, m_send, m_recv,
 ):
     ka = lax.axis_index("ka")
@@ -53,9 +53,8 @@
     barrier = pltpu.get_barrier_semaphore()
     for k in range(1, 8):
         say(barrier, in_row((row + k) % 8))
-    for k in range(1, 4):
-        say(barrier, in_plane(((yy + k) % 4) * 4 + zz))
-        say(barrier, in_plane(yy * 4 + (zz + k) % 4))
+    for k in range(1, 16):
+        say(barrier, in_plane((plane + k) % 16))
     loads = [pltpu.make_async_copy(h, v, in_sem.at[n]) for n, (h, v) in enumerate(((up_hbm, up_ref), (low_hbm, low_ref)))]
     dips = [pltpu.make_async_copy(h, dip.at[n], dip_sem.at[n]) for n, h in enumerate((dz_hbm, dr_hbm, dl_hbm))]
     for c in loads + dips:
@@ -78,7 +77,7 @@
                 for r in range(3):
                     value = jnp.where(owned[o][r], runs[r], value)
                 if u == 0:
-                    up_send[o * 2 + x2, w2] = value.astype(BF16)
+                    up_send[w2 * 8 + o * 2 + x2] = value.astype(BF16)
                 else:
                     low_send[w2, o * 2 + x2, u - 1] = value.astype(BF16)
         return 0
@@ -91,25 +90,42 @@
         return 0
 
     lax.fori_loop(0, 4, clear, 0)
-    pl.semaphore_wait(barrier, 13)
+    pl.semaphore_wait(barrier, 22)
+
+    def give_up(w, p):
+        send(up_send.at[w * 8 + p], up_recv.at[plane * 8 + row], s1.at[0], r1.at[0], (p // 2, (w // 4) * 8 + (p % 2) * 4 + w % 4))
 
     for k in range(1, 8):
-        p = (row + k) % 8
-        send(up_send.at[p], up_mid.at[row], s1.at[0], r1.at[0], in_row(p))
-    for k in range(1, 4):
-        say(ready, in_plane(yy * 4 + (zz + k) % 4))
-    up_mid[row] = up_send[row]
-    pl.semaphore_wait(ready, 3)
+        say(ready, in_row((row + k) % 8))
     for k in range(1, 16):
         w = (plane + k) % 16
         send(low_send.at[w], low_mid.at[plane], s1.at[1], r1.at[1], in_plane(w))
-    take(up_mid.at[pl.ds(0, 7)], r1.at[0])
-    for k in range(1, 16):
-        w = (plane + k) % 16
-        send(up_mid.at[:, w], up_recv.at[plane], s2.at[0], r2.at[0], in_plane(w))
-    up_recv[plane] = up_mid[:, plane]
+
+    def give_plane(k, _):
+        give_up((plane + k) % 16, row)
+        return 0
+
+    def give_row(k, _):
+        give_up(plane, (row + k) % 8)
+        return 0
+
+    lax.fori_loop(1, 16, give_plane, 0)
+    lax.fori_loop(1, 8, give_row, 0)
+    pl.semaphore_wait(ready, 7)
+
+    def give_rest(k, _):
+        give_up((plane + 1 + k // 7) % 16, (row + 1 + k % 7) % 8)
+        return 0
+
+    lax.fori_loop(0, 105, give_rest, 0)
+    up_recv[plane * 8 + row] = up_send[plane * 8 + row]
     low_mid[plane] = low_send[plane]
-    take(up_recv.at[pl.ds(0, 15)], r2.at[0])
+    take(low_mid.at[pl.ds(0, 15)], r1.at[1])
+    for k in range(1, 8):
+        p = (row + k) % 8
+        send(low_mid.at[:, p], low_recv.at[:, row], s2.at[1], r2.at[1], in_row(p))
+    low_recv[:, row] = low_mid[:, row]
+    take(up_recv.at[pl.ds(0, 127)], r1.at[0])
 
     lives = [live_ref[2 * ka + b] for b in range(2)]
 
@@ -119,7 +135,7 @@
             halves = []
             for b in range(2):
                 s = src_ref[ka * 128 + b * 64 + block]
-                tile = up_recv[s // 8, s % 8].astype(F32)
+                tile = up_recv[s].astype(F32)
                 halves.append(jnp.where(lane + block * 128 < lives[b], tile, 0.0))
             both = jnp.concatenate(halves, axis=0).astype(BF16)
             for c in range(4):
@@ -151,13 +167,15 @@
                     [jnp.where(keep, low_recv[s // 8, s % 8, u].astype(F32), 0.0) for u in range(2)], axis=0
                 ).astype(BF16)
                 at = b * 256 + h * 128
-                stage_low[v, :, at:at + 128] = both
-        return 0
-
-    def spread_low(k, _):
-        v2 = (vert + k) % 32
-        send(stage_low.at[v2], low_all.at[ka, vert], l_send, l_recv, (ka, v2))
-        return 0
+                stage_low[(v // 8) * 4 + v % 4, (v // 4) % 2, :, at:at + 128] = both
+        return 0
+
+    take(low_recv.at[:, pl.ds(0, 7)], r2.at[1])
+    lax.fori_loop(0, 32, arrange_low, 0)
+    for k in range(1, 16):
+        w = (plane + k) % 16
+        send(stage_low.at[w], low_plane.at[plane], l_send, l_recv, in_plane(w))
+    low_plane[plane] = stage_low[plane]
 
     def vid(y, x, z):
         return y * 8 + x * 4 + z
@@ -229,28 +247,27 @@
         cut = first
         here = where[second]
         middle = both(second, {}, first)
-        batches = [({second: here}, both(last, {}, first))]
+        if last == "x":
+            batches = both(last, {second: here}, first)
         yield
         on = onward(middle, second, {}, first, cut)
-        for step in (3, 1):
-            at = {second: (here + step) % 4}
-            batches.append((at, both(last, at, first)))
+        if last == "x":
+            for step in (3, 1):
+                batches += both(last, {second: (here + step) % 4}, first)
         yield
         for copy in on:
             copy.wait_recv()
-        at = {second: (here + 2) % 4}
-        batches.append((at, both(last, at, first)))
-        yield
         if last == "x":
-            for _, copies in batches:
-                copies[0].wait_recv()
+            batches += both(last, {second: (here + 2) % 4}, first)
+            yield
+            for copy in batches:
+                copy.wait_recv()
             yield
             return
-        ends = []
-        for group in (batches[:1], batches[1:3], batches[3:]):
-            for at, copies in group:
-                ends.extend(onward(copies, last, at, first, "x"))
-            yield
+        ends = both(last, {}, first + second)
+        yield
+        ends = onward(ends, last, {}, first + second, second)
+        yield
         for copy in ends:
             copy.wait_recv()
         yield
@@ -261,14 +278,15 @@
         for c in names:
             next(chains[c])
 
-    def low_copy(slot, owner, to):
-        return pltpu.make_async_remote_copy(
-            src_ref=low_all.at[owner], dst_ref=low_all.at[owner],
-            send_sem=m_send.at[slot], recv_sem=m_recv.at[slot], device_id=(to, vert), device_id_type=MESH,
+    core, side = ka % 2, ka // 2
+    sibling = side * 2 + 1 - core
+
+    def low_out(slot, h, x):
+        return send(
+            low_plane.at[:, x], low_all.at[core, side, xx], m_send.at[slot], m_recv.at[slot],
+            (h * 2 + core, yy * 8 + x * 4 + zz),
         )
 
-    sibling = (ka // 2) * 2 + (ka + 1) % 2
-    across = (ka + 2) % 4
     moves = []
     def term(c, n, rows):
         flat = rows.reshape(-1, WIDTHS[c])
@@ -304,31 +322,21 @@
         run(c)
     run(2, 3)
     run(0, 1)
-    take(low_mid.at[pl.ds(0, 15)], r1.at[1])
-    for k in range(1, 8):
-        p = (row + k) % 8
-        send(low_mid.at[:, p], low_recv.at[:, row], s2.at[1], r2.at[1], in_row(p))
-    low_recv[:, row] = low_mid[:, row]
     run(2, 3)
     run(0, 1)
-    take(low_recv.at[:, pl.ds(0, 7)], r2.at[1])
-    lax.fori_loop(0, 32, arrange_low, 0)
-    lax.fori_loop(1, 32, spread_low, 0)
-    low_all[ka, vert] = stage_low[vert]
+    take(low_plane.at[pl.ds(0, 15)], l_recv)
+    moves.append(low_out(0, side, 1 - xx))
+    moves.append(low_out(1, 1 - side, 1 - xx))
+    moves.append(low_out(2, 1 - side, xx))
+    low_all[core, side, xx] = low_plane[:, xx]
     run(2, 3)
-    run(0, 1)
     run(0, 1)
     run(2, 3)
     for c in dips:
         c.wait()
-    take(low_all.at[0, pl.ds(0, 31)], l_recv)
-    moves.append(low_copy(0, ka, sibling))
-    moves.append(low_copy(1, ka, across))
-    for m in moves:
-        m.start()
-    run(0, 1)
     add_z(zz)
     add_y(yy)
+    add_x(xx)
     run(0, 1)
 
     def sides(k, _):
@@ -337,18 +345,18 @@
         return 0
 
     lax.fori_loop(0, 2, sides, 0)
-    add_x(xx)
-    moves[1].wait_recv()
-    moves.append(low_copy(2, across, sibling))
-    moves[2].start()
     run(2, 3)
     add_x(1 - xx)
+    for m in moves:
+        m.wait_recv()
+    moves.append(send(
+        low_all.at[core], low_all.at[core], m_send.at[3], m_recv.at[3], (sibling, vert)
+    ))
     run(0)
     add_z((zz + 2) % 4)
     run(1)
     add_y((yy + 2) % 4)
-    moves[0].wait_recv()
-    moves[2].wait_recv()
+    moves[3].wait_recv()
 
     def factor(k, d):
         return rot_ref[d, k] * coup_ref[d, k].astype(F32)
@@ -369,17 +377,27 @@
 
     lax.fori_loop(0, 8, step, 0)
 
-    for t in range(4):
+    def amplitude(c, h):
+        quarter = (h * 2 + c) * 4
         total = None
         for o in range(4):
-            lows = low_all[o, pl.ds(t * 8, 8)].reshape(128, 512)
-            term = lax.dot_general(half[:, o * 512:(o + 1) * 512], lows, NT, preferred_element_type=F32)
-            total = term if total is None else total + term
-        tiles = total.reshape(32, 8, 128)
-        amp[t % 2, t // 2] = tiles
-
-    core, side = ka % 2, ka // 2
+            lows = low_all[o % 2, o // 2, :, pl.ds(quarter, 4)].reshape(128, 512)
+            value = lax.dot_general(half[:, o * 512:(o + 1) * 512], lows, NT, preferred_element_type=F32)
+            total = value if total is None else total + value
+        amp[c, h] = total.reshape(32, 8, 128)
+
+    def others(h, _):
+        amplitude(1 - core, h)
+        return 0
+
+    def own(h, _):
+        amplitude(core, h)
+        return 0
+
+    lax.fori_loop(0, 2, others, 0)
     to_pair = send(amp.at[1 - core], pair, s1.at[2], r1.at[2], (sibling, vert))
+    lax.fori_loop(0, 2, own, 0)
+
     to_pair.wait_recv()
     pair[...] = pair[...] + amp[core]
     mine = side * 32 + vert
@@ -395,14 +413,13 @@
     total = jnp.sum(part[...], axis=0)
     out_ref[...] = total * total
 
-    take(up_send.at[pl.ds(0, 7)], s1.at[0])
-    take(up_recv.at[pl.ds(0, 15)], s2.at[0])
+    take(up_send.at[pl.ds(0, 127)], s1.at[0])
     take(low_send.at[pl.ds(0, 15)], s1.at[1])
     take(low_recv.at[:, pl.ds(0, 7)], s2.at[1])
     for copies in exchanges:
         for copy in copies:
             copy.wait_send()
-    take(stage_low.at[pl.ds(0, 31)], l_send)
+    take(stage_low.at[pl.ds(0, 15)], l_send)
     for copy in sent + moves:
         copy.wait_send()
     to_pair.wait_send()
@@ -429,16 +446,16 @@
         scratch_shapes=[
             pltpu.VMEM((64, 8, 512), BF16),
             pltpu.VMEM((32, 8, 512), BF16),
-            pltpu.VMEM((8, 16, 8, 128), BF16),
-            pltpu.VMEM((8, 16, 8, 128), BF16),
-            pltpu.VMEM((16, 8, 8, 128), BF16),
+            pltpu.VMEM((128, 8, 128), BF16),
+            pltpu.VMEM((128, 8, 128), BF16),
             pltpu.VMEM((16, 8, 2, 8, 128), BF16),
             pltpu.VMEM((16, 8, 2, 8, 128), BF16),
             pltpu.VMEM((16, 8, 2, 8, 128), BF16),
             *[pltpu.VMEM((4, 16, w), BF16) for w in WIDTHS],
             *[pltpu.VMEM((4, 2, 4, 4, 16, w), BF16) for w in WIDTHS],
-            pltpu.VMEM((32, 16, 512), BF16),
-            pltpu.VMEM((4, 32, 16, 512), BF16),
+            pltpu.VMEM((16, 2, 16, 512), BF16),
+            pltpu.VMEM((16, 2, 16, 512), BF16),
+            pltpu.VMEM((2, 2, 2, 16, 16, 512), BF16),
             pltpu.VMEM((3, 256, 2048), BF16),
             pltpu.VMEM((3, 4, 2, 4, 64, 256), F32),
             pltpu.VMEM((256, 2048), BF16),
@@ -451,7 +468,7 @@
             dma((4, 3)), dma((4, 3)),
             dma((4, 24)), dma((4, 24)),
             dma, dma,
-            dma((3,)), dma((3,)),
+            dma((4,)), dma((4,)),
         ],
         compiler_params=pltpu.CompilerParams(
             collective_id=0, has_side_effects=True, vmem_limit_bytes=60 * 1024 * 1024

time: 102 us -> 100 us (0.980)
  Pallas kernels: 99.1 us -> 96.7 us
    pallas_call x1, Pallas kernels: 99.1 us -> 96.7 us  [per_device(): pl.pallas_call(kernel, out_shape=jax.ShapeDtypeStruct((8, 128), F32), in_...]
where the time goes in v4:
time: 100 us; the launch traced here: 99.9 us
  Pallas kernels  96.7 us (97%)
  local copies, waits for them, and re-layouts  2.37 us (2%)
    pallas_call x1, Pallas kernels, per_device(): pl.pallas_call(kernel, out_shape=jax.ShapeDtypeStruct((8, 128), F32), in_...  96.7 us

profile of v4, /device:TPU:1, one launch (start us, length us, event | category | flops | bytes accessed | tf_op | source)
XLA Modules:
  0.0 99.9 jit_solution(12527589492183184580)
XLA Ops:
  0.0 1.1 %slice_reduce_fusion = s32[512]{0:T(512)S(1)} fusion(s32[512,128]{1,0:T(8,128)} %bitcast.6), kind=kLoop, calls=%fused_computation.2 | loop fusion | bytes 4096 | tf_op jit(solution)/shard_map/slice | solution.py:432
  1.1 0.0 copy-start
  1.1 0.8 select_reduce_fusion.src_ref
  1.9 0.0 copy-done
  1.9 96.7 %shard_map.91 = f32[8,128]{1,0:T(8,128)} custom-call(s32[512]{0:T(512)} %copy-done, s32[512]{0:T(512)} %select_reduce_fusion.src_ref, s32[8]{0:T(128)} %live_ref.1, s32[3,8]{1,0:T(4,128)} %bitcast.10, f32[3,8]{1,0:T(4,128)} %bitcast.11, bf16[64,8,512]{2,1,0:T(8,128)(2,1)} %bitcast.8, bf16[32,8,512]{2,1,0:T(8,128)(2,1)} %bitcast.9, bf16[256,2048]{1,0:T(8,128)(2,1)} %dz_hbm.1, ...), custom_call_target="tpu_custom_call" | custom-call | flops 7000000000 | bytes 5000000 | tf_op jit(solution)/shard_map/pallas_call | solution.py:441
  98.6 1.3 %copy.11 = f32[128,8]{0,1:T(8,128)} copy(f32[128,8]{0,1:T(8,128)} %bitcast.7) | data formatting | bytes 8192
  (1 shorter events, 0.0 us)
Async XLA Ops:
  1.1 0.8 copy-start

commit v5 on v4

--- a/solution.py
+++ b/solution.py
@@ -8,9 +8,10 @@
 F32 = jnp.float32
 BF16 = jnp.bfloat16
 MESH = pl.DeviceIdType.MESH
-WIDTHS = (768, 768, 256, 256)
-STARTS = (0, 768, 1536, 1792)
-ORDERS = ("xyz", "xzy", "yzx", "zyx")
+WIDTHS = (512, 512, 256, 256, 256, 256)
+STARTS = (0, 512, 1024, 1280, 1536, 1792)
+ORDERS = ("xyz", "xzy", "yzx", "zyx", "xyz", "xzy")
+CHAINS = len(WIDTHS)
 NT = (((1,), (1,)), ((), ()))
 
 
@@ -18,7 +19,7 @@
     head_ref, src_ref, live_ref, coup_ref, rot_ref, low_hbm, up_hbm, dz_hbm, dr_hbm, dl_hbm,
     out_ref,
     low_ref, up_ref, up_send, up_recv, low_send, low_mid, low_recv,
-    sta, stb, stc, std_, ua, ub, uc, ud, stage_low, low_plane, low_all, dip, acc, half, amp, pair, part,
+    sta, stb, stc, std_, ste, stf, ua, ub, uc, ud, ue, uf, stage_low, low_plane, low_all, dip, acc, half, amp, pair, part,
     ready, in_sem, dip_sem, s1, r1, s2, r2, q_send, q_recv, g_send, g_recv, l_send, l_recv, m_send, m_recv,
 ):
     ka = lax.axis_index("ka")
@@ -28,8 +29,8 @@
     zz = vert % 4
     row = ka * 2 + xx
     plane = yy * 4 + zz
-    stages = (sta, stb, stc, std_)
-    uppers = (ua, ub, uc, ud)
+    stages = (sta, stb, stc, std_, ste, stf)
+    uppers = (ua, ub, uc, ud, ue, uf)
 
     def in_row(p):
         return p // 2, yy * 8 + (p % 2) * 4 + zz
@@ -51,10 +52,15 @@
         return copy
 
     barrier = pltpu.get_barrier_semaphore()
-    for k in range(1, 8):
-        say(barrier, in_row((row + k) % 8))
-    for k in range(1, 16):
-        say(barrier, in_plane((plane + k) % 16))
+    def each(count, body):
+        def step(k, _):
+            body(k)
+            return 0
+
+        lax.fori_loop(1, count, step, 0)
+
+    each(8, lambda k: say(barrier, in_row((row + k) % 8)))
+    each(16, lambda k: say(barrier, in_plane((plane + k) % 16)))
     loads = [pltpu.make_async_copy(h, v, in_sem.at[n]) for n, (h, v) in enumerate(((up_hbm, up_ref), (low_hbm, low_ref)))]
     dips = [pltpu.make_async_copy(h, dip.at[n], dip_sem.at[n]) for n, h in enumerate((dz_hbm, dr_hbm, dl_hbm))]
     for c in loads + dips:
@@ -95,11 +101,7 @@
     def give_up(w, p):
         send(up_send.at[w * 8 + p], up_recv.at[plane * 8 + row], s1.at[0], r1.at[0], (p // 2, (w // 4) * 8 + (p % 2) * 4 + w % 4))
 
-    for k in range(1, 8):
-        say(ready, in_row((row + k) % 8))
-    for k in range(1, 16):
-        w = (plane + k) % 16
-        send(low_send.at[w], low_mid.at[plane], s1.at[1], r1.at[1], in_plane(w))
+    each(8, lambda k: say(ready, in_row((row + k) % 8)))
 
     def give_plane(k, _):
         give_up((plane + k) % 16, row)
@@ -119,13 +121,14 @@
 
     lax.fori_loop(0, 105, give_rest, 0)
     up_recv[plane * 8 + row] = up_send[plane * 8 + row]
+    take(up_recv.at[pl.ds(0, 127)], r1.at[0])
+
+    def give_mid(k):
+        w = (plane + k) % 16
+        send(low_send.at[w], low_mid.at[plane], s1.at[1], r1.at[1], in_plane(w))
+
+    each(16, give_mid)
     low_mid[plane] = low_send[plane]
-    take(low_mid.at[pl.ds(0, 15)], r1.at[1])
-    for k in range(1, 8):
-        p = (row + k) % 8
-        send(low_mid.at[:, p], low_recv.at[:, row], s2.at[1], r2.at[1], in_row(p))
-    low_recv[:, row] = low_mid[:, row]
-    take(up_recv.at[pl.ds(0, 127)], r1.at[0])
 
     lives = [live_ref[2 * ka + b] for b in range(2)]
 
@@ -138,7 +141,7 @@
                 tile = up_recv[s].astype(F32)
                 halves.append(jnp.where(lane + block * 128 < lives[b], tile, 0.0))
             both = jnp.concatenate(halves, axis=0).astype(BF16)
-            for c in range(4):
+            for c in range(CHAINS):
                 if STARTS[c] <= n * 128 < STARTS[c] + WIDTHS[c]:
                     at = n * 128 - STARTS[c]
                     stages[c][q, :, at:at + 128] = both
@@ -146,15 +149,14 @@
 
     lax.fori_loop(0, 4, arrange_up, 0)
 
-    exchanges = []
-    for c in range(4):
-        copies = []
+    order = (4, 5, 2, 3, 0, 1)
+
+    for c in order:
         for d in range(1, 4):
             q = (ka + d) % 4
-            copies.append(send(
-                stages[c].at[q], uppers[c].at[yy, xx, zz, ka], q_send.at[c, d - 1], q_recv.at[c, d - 1], (q, vert)
-            ))
-        exchanges.append(copies)
+            send(
+                stages[c].at[q], uppers[c].at[yy, xx, zz, ka], q_send.at[c], q_recv.at[c], (q, vert)
+            )
         uppers[c][yy, xx, zz, ka] = stages[c][ka]
 
     def arrange_low(v, _):
@@ -169,13 +171,6 @@
                 at = b * 256 + h * 128
                 stage_low[(v // 8) * 4 + v % 4, (v // 4) % 2, :, at:at + 128] = both
         return 0
-
-    take(low_recv.at[:, pl.ds(0, 7)], r2.at[1])
-    lax.fori_loop(0, 32, arrange_low, 0)
-    for k in range(1, 16):
-        w = (plane + k) % 16
-        send(stage_low.at[w], low_plane.at[plane], l_send, l_recv, in_plane(w))
-    low_plane[plane] = stage_low[plane]
 
     def vid(y, x, z):
         return y * 8 + x * 4 + z
@@ -272,7 +267,7 @@
             copy.wait_recv()
         yield
 
-    chains = [chain(c) for c in range(4)]
+    chains = [chain(c) for c in range(CHAINS)]
 
     def run(*names):
         for c in names:
@@ -297,14 +292,14 @@
 
     def add_z(z):
         def body(n, _):
-            acc[n, :, :, z] += term(0, n, ua[:, :, z]).reshape(4, 2, 64, 256)
+            acc[n, :, :, z] += (term(0, n, ua[:, :, z]) + term(4, n, ue[:, :, z])).reshape(4, 2, 64, 256)
             return 0
 
         lax.fori_loop(0, 3, body, 0)
 
     def add_y(y):
         def body(n, _):
-            acc[n, y] += term(1, n, ub[y]).reshape(2, 4, 64, 256)
+            acc[n, y] += (term(1, n, ub[y]) + term(5, n, uf[y])).reshape(2, 4, 64, 256)
             return 0
 
         lax.fori_loop(0, 3, body, 0)
@@ -316,26 +311,46 @@
 
         lax.fori_loop(0, 3, body, 0)
 
-    for c in (2, 3, 0, 1):
-        for copy in exchanges[c]:
-            copy.wait_recv()
+    for c in order:
+        take(stages[c].at[pl.ds(0, 3)], q_recv.at[c])
         run(c)
+    run(4, 5)
+    run(2, 3)
+    run(0, 1)
+    run(4, 5)
+    take(low_mid.at[pl.ds(0, 15)], r1.at[1])
+
+    def give_low(k):
+        p = (row + k) % 8
+        send(low_mid.at[:, p], low_recv.at[:, row], s2.at[1], r2.at[1], in_row(p))
+
+    each(8, give_low)
+    low_recv[:, row] = low_mid[:, row]
+    run(2, 3)
+    run(4, 5)
+    run(0, 1)
     run(2, 3)
     run(0, 1)
     run(2, 3)
-    run(0, 1)
+    take(low_recv.at[:, pl.ds(0, 7)], r2.at[1])
+    lax.fori_loop(0, 32, arrange_low, 0)
+
+    def give_rows(k):
+        w = (plane + k) % 16
+        send(stage_low.at[w], low_plane.at[plane], l_send, l_recv, in_plane(w))
+
+    each(16, give_rows)
+    low_plane[plane] = stage_low[plane]
+    for c in dips:
+        c.wait()
+    add_z(zz)
+    add_y(yy)
+    run(4, 5)
     take(low_plane.at[pl.ds(0, 15)], l_recv)
     moves.append(low_out(0, side, 1 - xx))
     moves.append(low_out(1, 1 - side, 1 - xx))
     moves.append(low_out(2, 1 - side, xx))
     low_all[core, side, xx] = low_plane[:, xx]
-    run(2, 3)
-    run(0, 1)
-    run(2, 3)
-    for c in dips:
-        c.wait()
-    add_z(zz)
-    add_y(yy)
     add_x(xx)
     run(0, 1)
 
@@ -352,9 +367,9 @@
     moves.append(send(
         low_all.at[core], low_all.at[core], m_send.at[3], m_recv.at[3], (sibling, vert)
     ))
-    run(0)
+    run(4, 0)
     add_z((zz + 2) % 4)
-    run(1)
+    run(5, 1)
     add_y((yy + 2) % 4)
     moves[3].wait_recv()
 
@@ -409,21 +424,19 @@
 
     lax.fori_loop(1, 64, give, 0)
     part[mine] = pair[side, vert]
-    take(part.at[pl.ds(0, 63)], r2.at[2])
-    total = jnp.sum(part[...], axis=0)
-    out_ref[...] = total * total
-
     take(up_send.at[pl.ds(0, 127)], s1.at[0])
     take(low_send.at[pl.ds(0, 15)], s1.at[1])
     take(low_recv.at[:, pl.ds(0, 7)], s2.at[1])
-    for copies in exchanges:
-        for copy in copies:
-            copy.wait_send()
+    for c in order:
+        take(stages[c].at[pl.ds(0, 3)], q_send.at[c])
     take(stage_low.at[pl.ds(0, 15)], l_send)
     for copy in sent + moves:
         copy.wait_send()
     to_pair.wait_send()
     take(part.at[pl.ds(0, 63)], s2.at[2])
+    take(part.at[pl.ds(0, 63)], r2.at[2])
+    total = jnp.sum(part[...], axis=0)
+    out_ref[...] = total * total
 
 
 def per_device(
@@ -465,8 +478,8 @@
             pltpu.SemaphoreType.REGULAR,
             dma((2,)), dma((3,)),
             dma((3,)), dma((3,)), dma((3,)), dma((3,)),
-            dma((4, 3)), dma((4, 3)),
-            dma((4, 24)), dma((4, 24)),
+            dma((CHAINS,)), dma((CHAINS,)),
+            dma((CHAINS, 12)), dma((CHAINS, 12)),
             dma, dma,
             dma((4,)), dma((4,)),
         ],

time: 100 us -> 95.8 us (0.958)
  Pallas kernels: 96.7 us -> 92.4 us
    pallas_call x1, Pallas kernels: 96.7 us -> 92.4 us  [per_device(): pl.pallas_call(kernel, out_shape=jax.ShapeDtypeStruct((8, 128), F32), in_...]
where the time goes in v5:
time: 95.8 us; the launch traced here: 95.6 us
  Pallas kernels  92.4 us (96%)
  local copies, waits for them, and re-layouts  2.37 us (2%)
    pallas_call x1, Pallas kernels, per_device(): pl.pallas_call(kernel, out_shape=jax.ShapeDtypeStruct((8, 128), F32), in_...  92.4 us

profile of v5, /device:TPU:1, one launch (start us, length us, event | category | flops | bytes accessed | tf_op | source)
XLA Modules:
  0.0 95.6 jit_solution(6741424166773576375)
XLA Ops:
  0.0 1.1 %slice_reduce_fusion = s32[512]{0:T(512)S(1)} fusion(s32[512,128]{1,0:T(8,128)} %bitcast.6), kind=kLoop, calls=%fused_computation.2 | loop fusion | bytes 4096 | tf_op jit(solution)/shard_map/slice | solution.py:445
  1.1 0.0 copy-start
  1.1 0.8 select_reduce_fusion.src_ref
  1.9 0.0 copy-done
  1.9 92.4 %shard_map.91 = f32[8,128]{1,0:T(8,128)} custom-call(s32[512]{0:T(512)} %copy-done, s32[512]{0:T(512)} %select_reduce_fusion.src_ref, s32[8]{0:T(128)} %live_ref.1, s32[3,8]{1,0:T(4,128)} %bitcast.10, f32[3,8]{1,0:T(4,128)} %bitcast.11, bf16[64,8,512]{2,1,0:T(8,128)(2,1)} %bitcast.8, bf16[32,8,512]{2,1,0:T(8,128)(2,1)} %bitcast.9, bf16[256,2048]{1,0:T(8,128)(2,1)} %dz_hbm.1, ...), custom_call_target="tpu_custom_call" | custom-call | flops 7000000000 | bytes 5000000 | tf_op jit(solution)/shard_map/pallas_call | solution.py:454
  94.3 1.3 %copy.11 = f32[128,8]{0,1:T(8,128)} copy(f32[128,8]{0,1:T(8,128)} %bitcast.7) | data formatting | bytes 8192
  (1 shorter events, 0.0 us)
Async XLA Ops:
  1.1 0.8 copy-start

commit v6 on v5

--- a/solution.py
+++ b/solution.py
@@ -16,9 +16,9 @@
 
 
 def kernel(
-    head_ref, src_ref, live_ref, coup_ref, rot_ref, low_hbm, up_hbm, dz_hbm, dr_hbm, dl_hbm,
+    live_ref, coup_ref, rot_ref, map_hbm, low_hbm, up_hbm, dz_hbm, dr_hbm, dl_hbm,
     out_ref,
-    low_ref, up_ref, up_send, up_recv, low_send, low_mid, low_recv,
+    map_ref, table, src_ref, low_ref, up_ref, up_send, up_recv, low_send, low_mid, low_recv,
     sta, stb, stc, std_, ste, stf, ua, ub, uc, ud, ue, uf, stage_low, low_plane, low_all, dip, acc, half, amp, pair, part,
     ready, in_sem, dip_sem, s1, r1, s2, r2, q_send, q_recv, g_send, g_recv, l_send, l_recv, m_send, m_recv,
 ):
@@ -61,7 +61,7 @@
 
     each(8, lambda k: say(barrier, in_row((row + k) % 8)))
     each(16, lambda k: say(barrier, in_plane((plane + k) % 16)))
-    loads = [pltpu.make_async_copy(h, v, in_sem.at[n]) for n, (h, v) in enumerate(((up_hbm, up_ref), (low_hbm, low_ref)))]
+    loads = [pltpu.make_async_copy(h, v, in_sem.at[n]) for n, (h, v) in enumerate(((map_hbm, map_ref), (up_hbm, up_ref), (low_hbm, low_ref)))]
     dips = [pltpu.make_async_copy(h, dip.at[n], dip_sem.at[n]) for n, h in enumerate((dz_hbm, dr_hbm, dl_hbm))]
     for c in loads + dips:
         c.start()
@@ -70,7 +70,7 @@
 
     lane = lax.broadcasted_iota(jnp.int32, (8, 128), 1)
     zeros = jnp.zeros((8, 128), jnp.int32)
-    heads = [zeros + head_ref[(ka * 32 + vert) * 4 + r] for r in range(4)]
+    heads = [zeros + map_ref[pl.ds((ka * 32 + vert) * 4 + r, 1), :][:, 0:1] // 128 for r in range(4)]
     owned = [[(heads[r] >= o * 128) & (heads[r] < (o + 1) * 128) for r in range(3)] for o in range(4)]
 
     def pack(j, _):
@@ -121,6 +121,19 @@
 
     lax.fori_loop(0, 105, give_rest, 0)
     up_recv[plane * 8 + row] = up_send[plane * 8 + row]
+
+    def find(g, found):
+        block = map_ref[pl.ds(pl.multiple_of(g * 64, 64), 64), :][:, 0:1] // 128
+        run = lax.broadcasted_iota(jnp.int32, (64, 512), 0) + g * 64
+        device = run // 4
+        place = ((device // 8) % 4 * 4 + device % 4) * 8 + device // 32 * 2 + device // 4 % 2
+        hit = block == lax.broadcasted_iota(jnp.int32, (64, 512), 1)
+        return jnp.maximum(found, jnp.max(jnp.where(hit, place, 0), axis=0, keepdims=True))
+
+    table[...] = lax.fori_loop(0, 8, find, jnp.zeros((1, 512), jnp.int32))
+    to_scalars = pltpu.make_async_copy(table, src_ref, in_sem.at[3])
+    to_scalars.start()
+    to_scalars.wait()
     take(up_recv.at[pl.ds(0, 127)], r1.at[0])
 
     def give_mid(k):
@@ -137,7 +150,7 @@
             block = q * 16 + n
             halves = []
             for b in range(2):
-                s = src_ref[ka * 128 + b * 64 + block]
+                s = src_ref[0, ka * 128 + b * 64 + block]
                 tile = up_recv[s].astype(F32)
                 halves.append(jnp.where(lane + block * 128 < lives[b], tile, 0.0))
             both = jnp.concatenate(halves, axis=0).astype(BF16)
@@ -151,19 +164,23 @@
 
     order = (4, 5, 2, 3, 0, 1)
 
+    def pieces(c):
+        return 7 if ORDERS[c][0] == "x" else 3
+
     for c in order:
-        for d in range(1, 4):
-            q = (ka + d) % 4
-            send(
-                stages[c].at[q], uppers[c].at[yy, xx, zz, ka], q_send.at[c], q_recv.at[c], (q, vert)
-            )
+        for k in range(1, 8):
+            p = (row + k) % 8
+            if ORDERS[c][0] != "x":
+                if k % 2:
+                    continue
+            send(stages[c].at[p // 2], uppers[c].at[yy, xx, zz, ka], q_send.at[c], q_recv.at[c], in_row(p))
         uppers[c][yy, xx, zz, ka] = stages[c][ka]
 
     def arrange_low(v, _):
         for b in range(2):
             for h in range(2):
                 block = 2 * v + h
-                s = src_ref[ka * 128 + b * 64 + block]
+                s = src_ref[0, ka * 128 + b * 64 + block]
                 keep = lane + block * 128 < lives[b]
                 both = jnp.concatenate(
                     [jnp.where(keep, low_recv[s // 8, s % 8, u].astype(F32), 0.0) for u in range(2)], axis=0
@@ -230,11 +247,9 @@
                 out.append(go(ref, axis, step))
             return out
 
-        begun = both(first, {}, "")
-        yield
-        if first == "x":
-            begun[0].wait_recv()
-        else:
+        if first != "x":
+            begun = both(first, {}, "")
+            yield
             on = onward(begun, first, {}, "", "o")
             yield
             for copy in on:
@@ -312,8 +327,9 @@
         lax.fori_loop(0, 3, body, 0)
 
     for c in order:
-        take(stages[c].at[pl.ds(0, 3)], q_recv.at[c])
+        take(stages[c].at[pl.ds(0, pieces(c))], q_recv.at[c])
         run(c)
+    run(2, 3)
     run(4, 5)
     run(2, 3)
     run(0, 1)
@@ -326,9 +342,6 @@
 
     each(8, give_low)
     low_recv[:, row] = low_mid[:, row]
-    run(2, 3)
-    run(4, 5)
-    run(0, 1)
     run(2, 3)
     run(0, 1)
     run(2, 3)
@@ -428,7 +441,7 @@
     take(low_send.at[pl.ds(0, 15)], s1.at[1])
     take(low_recv.at[:, pl.ds(0, 7)], s2.at[1])
     for c in order:
-        take(stages[c].at[pl.ds(0, 3)], q_send.at[c])
+        take(stages[c].at[pl.ds(0, pieces(c))], q_send.at[c])
     take(stage_low.at[pl.ds(0, 15)], l_send)
     for copy in sent + moves:
         copy.wait_send()
@@ -442,11 +455,6 @@
 def per_device(
     eig_lower, eig_upper, layout_map, block_live, coupling, rot_coef, dip_zero, dip_raise, dip_lower
 ):
-    heads = layout_map.reshape(512, 128)[:, 0] // 128
-    hits = heads[None, :] == jnp.arange(512, dtype=jnp.int32)[:, None]
-    device = jnp.arange(512, dtype=jnp.int32) // 4
-    place = ((device // 8) % 4 * 4 + device % 4) * 8 + device // 32 * 2 + device // 4 % 2
-    source = jnp.sum(jnp.where(hits, place[None, :], 0), axis=1)
     smem = pl.BlockSpec(memory_space=pltpu.SMEM)
     vmem = pl.BlockSpec(memory_space=pltpu.VMEM)
     hbm = pl.BlockSpec(memory_space=pl.ANY)
@@ -454,9 +462,12 @@
     out = pl.pallas_call(
         kernel,
         out_shape=jax.ShapeDtypeStruct((8, 128), F32),
-        in_specs=[smem] * 5 + [hbm] * 5,
+        in_specs=[smem] * 3 + [hbm] * 6,
         out_specs=vmem,
         scratch_shapes=[
+            pltpu.VMEM((512, 128), jnp.int32),
+            pltpu.VMEM((1, 512), jnp.int32),
+            pltpu.SMEM((1, 512), jnp.int32),
             pltpu.VMEM((64, 8, 512), BF16),
             pltpu.VMEM((32, 8, 512), BF16),
             pltpu.VMEM((128, 8, 128), BF16),
@@ -464,7 +475,7 @@
             pltpu.VMEM((16, 8, 2, 8, 128), BF16),
             pltpu.VMEM((16, 8, 2, 8, 128), BF16),
             pltpu.VMEM((16, 8, 2, 8, 128), BF16),
-            *[pltpu.VMEM((4, 16, w), BF16) for w in WIDTHS],
+            *[pltpu.VMEM((8, 16, w), BF16) for w in WIDTHS],
             *[pltpu.VMEM((4, 2, 4, 4, 16, w), BF16) for w in WIDTHS],
             pltpu.VMEM((16, 2, 16, 512), BF16),
             pltpu.VMEM((16, 2, 16, 512), BF16),
@@ -476,7 +487,7 @@
             pltpu.VMEM((2, 32, 8, 128), F32),
             pltpu.VMEM((64, 8, 128), F32),
             pltpu.SemaphoreType.REGULAR,
-            dma((2,)), dma((3,)),
+            dma((4,)), dma((3,)),
             dma((3,)), dma((3,)), dma((3,)), dma((3,)),
             dma((CHAINS,)), dma((CHAINS,)),
             dma((CHAINS, 12)), dma((CHAINS, 12)),
@@ -488,7 +499,7 @@
         ),
         cost_estimate=pl.CostEstimate(flops=7_000_000_000, bytes_accessed=5_000_000, transcendentals=0),
     )(
-        heads, source, block_live, coupling.T, rot_coef.T,
+        block_live, coupling.T, rot_coef.T, layout_map.reshape(512, 128),
         eig_lower.reshape(64, 8, 512), eig_upper.reshape(32, 8, 512), dip_zero, dip_raise, dip_lower,
     )
     return out.T

time: 95.8 us -> 94.4 us (0.985)
  local copies, waits for them, and re-layouts: 2.37 us -> 1.28 us
    slice x1 -> x0, local copies, waits for them, and re-layouts: 1.09 us -> none  [per_device(): heads = layout_map.reshape(512, 128)[:, 0] // 128]
where the time goes in v6:
time: 94.4 us; the launch traced here: 94.2 us
  Pallas kernels  92.9 us (98%)
  local copies, waits for them, and re-layouts  1.28 us (1%)
    pallas_call x1, Pallas kernels, per_device(): pl.pallas_call(kernel, out_shape=jax.ShapeDtypeStruct((8, 128), F32), in_...  92.9 us

profile of v6, /device:TPU:1, one launch (start us, length us, event | category | flops | bytes accessed | tf_op | source)
XLA Modules:
  0.0 94.2 jit_solution(13758466213586049146)
XLA Ops:
  0.0 92.9 %shard_map.91 = f32[8,128]{1,0:T(8,128)} custom-call(s32[8]{0:T(128)} %live_ref.1, s32[3,8]{1,0:T(4,128)} %bitcast.10, f32[3,8]{1,0:T(4,128)} %bitcast.11, s32[512,128]{1,0:T(8,128)} %bitcast.8, bf16[64,8,512]{2,1,0:T(8,128)(2,1)} %bitcast.7, bf16[32,8,512]{2,1,0:T(8,128)(2,1)} %bitcast.9, bf16[256,2048]{1,0:T(8,128)(2,1)} %dz_hbm.1, ...), custom_call_target="tpu_custom_call" | custom-call | flops 7000000000 | bytes 5000000 | tf_op jit(solution)/shard_map/pallas_call | solution.py:462
  92.9 1.3 %copy.11 = f32[128,8]{0,1:T(8,128)} copy(f32[128,8]{0,1:T(8,128)} %bitcast.6) | data formatting | bytes 8192

commit v7 on v6

--- a/solution.py
+++ b/solution.py
@@ -120,6 +120,13 @@
         return 0
 
     lax.fori_loop(0, 105, give_rest, 0)
+
+    def give_mid(k):
+        w = (plane + k) % 16
+        send(low_send.at[w], low_mid.at[plane], s1.at[1], r1.at[1], in_plane(w))
+
+    each(16, give_mid)
+    low_mid[plane] = low_send[plane]
     up_recv[plane * 8 + row] = up_send[plane * 8 + row]
 
     def find(g, found):
@@ -135,13 +142,6 @@
     to_scalars.start()
     to_scalars.wait()
     take(up_recv.at[pl.ds(0, 127)], r1.at[0])
-
-    def give_mid(k):
-        w = (plane + k) % 16
-        send(low_send.at[w], low_mid.at[plane], s1.at[1], r1.at[1], in_plane(w))
-
-    each(16, give_mid)
-    low_mid[plane] = low_send[plane]
 
     lives = [live_ref[2 * ka + b] for b in range(2)]
 
@@ -162,7 +162,7 @@
 
     lax.fori_loop(0, 4, arrange_up, 0)
 
-    order = (4, 5, 2, 3, 0, 1)
+    order = (2, 3, 4, 5, 0, 1)
 
     def pieces(c):
         return 7 if ORDERS[c][0] == "x" else 3
@@ -326,6 +326,14 @@
 
         lax.fori_loop(0, 3, body, 0)
 
+    take(low_mid.at[pl.ds(0, 15)], r1.at[1])
+
+    def give_low(k):
+        p = (row + k) % 8
+        send(low_mid.at[:, p], low_recv.at[:, row], s2.at[1], r2.at[1], in_row(p))
+
+    each(8, give_low)
+    low_recv[:, row] = low_mid[:, row]
     for c in order:
         take(stages[c].at[pl.ds(0, pieces(c))], q_recv.at[c])
         run(c)
@@ -333,27 +341,19 @@
     run(4, 5)
     run(2, 3)
     run(0, 1)
+    take(low_recv.at[:, pl.ds(0, 7)], r2.at[1])
+    lax.fori_loop(0, 32, arrange_low, 0)
+
+    def give_rows(k):
+        w = (plane + k) % 16
+        send(stage_low.at[w], low_plane.at[plane], l_send, l_recv, in_plane(w))
+
+    each(16, give_rows)
+    low_plane[plane] = stage_low[plane]
     run(4, 5)
-    take(low_mid.at[pl.ds(0, 15)], r1.at[1])
-
-    def give_low(k):
-        p = (row + k) % 8
-        send(low_mid.at[:, p], low_recv.at[:, row], s2.at[1], r2.at[1], in_row(p))
-
-    each(8, give_low)
-    low_recv[:, row] = low_mid[:, row]
     run(2, 3)
     run(0, 1)
     run(2, 3)
-    take(low_recv.at[:, pl.ds(0, 7)], r2.at[1])
-    lax.fori_loop(0, 32, arrange_low, 0)
-
-    def give_rows(k):
-        w = (plane + k) % 16
-        send(stage_low.at[w], low_plane.at[plane], l_send, l_recv, in_plane(w))
-
-    each(16, give_rows)
-    low_plane[plane] = stage_low[plane]
     for c in dips:
         c.wait()
     add_z(zz)

time: 94.4 us -> 88.8 us (0.941)
  Pallas kernels: 92.9 us -> 87.4 us
    pallas_call x1, Pallas kernels: 92.9 us -> 87.4 us  [per_device(): pl.pallas_call(kernel, out_shape=jax.ShapeDtypeStruct((8, 128), F32), in_...]
where the time goes in v7:
time: 88.8 us; the launch traced here: 88.7 us
  Pallas kernels  87.4 us (98%)
  local copies, waits for them, and re-layouts  1.28 us (1%)
    pallas_call x1, Pallas kernels, per_device(): pl.pallas_call(kernel, out_shape=jax.ShapeDtypeStruct((8, 128), F32), in_...  87.4 us

profile of v7, /device:TPU:1, one launch (start us, length us, event | category | flops | bytes accessed | tf_op | source)
XLA Modules:
  0.0 88.7 jit_solution(14547015165897656011)
XLA Ops:
  0.0 87.4 %shard_map.91 = f32[8,128]{1,0:T(8,128)} custom-call(s32[8]{0:T(128)} %live_ref.1, s32[3,8]{1,0:T(4,128)} %bitcast.10, f32[3,8]{1,0:T(4,128)} %bitcast.11, s32[512,128]{1,0:T(8,128)} %bitcast.8, bf16[64,8,512]{2,1,0:T(8,128)(2,1)} %bitcast.7, bf16[32,8,512]{2,1,0:T(8,128)(2,1)} %bitcast.9, bf16[256,2048]{1,0:T(8,128)(2,1)} %dz_hbm.1, ...), custom_call_target="tpu_custom_call" | custom-call | flops 7000000000 | bytes 5000000 | tf_op jit(solution)/shard_map/pallas_call | solution.py:462
  87.4 1.3 %copy.11 = f32[128,8]{0,1:T(8,128)} copy(f32[128,8]{0,1:T(8,128)} %bitcast.6) | data formatting | bytes 8192

commit v8 on v7

--- a/solution.py
+++ b/solution.py
@@ -414,28 +414,25 @@
             total = value if total is None else total + value
         amp[c, h] = total.reshape(32, 8, 128)
 
-    def others(h, _):
+    to_pair = []
+    for n in range(2):
+        h = (side + n) % 2
         amplitude(1 - core, h)
-        return 0
-
-    def own(h, _):
+        to_pair.append(send(amp.at[1 - core, h], pair.at[h], s1.at[2 + n], r1.at[2 + n], (sibling, vert)))
+
+    mine = side * 32 + vert
+    for n in range(2):
+        h = (side + n) % 2
         amplitude(core, h)
-        return 0
-
-    lax.fori_loop(0, 2, others, 0)
-    to_pair = send(amp.at[1 - core], pair, s1.at[2], r1.at[2], (sibling, vert))
-    lax.fori_loop(0, 2, own, 0)
-
-    to_pair.wait_recv()
-    pair[...] = pair[...] + amp[core]
-    mine = side * 32 + vert
-
-    def give(k, _):
-        h2, v2 = (side + k // 32) % 2, (vert + k % 32) % 32
-        send(pair.at[h2, v2], part.at[mine], s2.at[2], r2.at[2], (h2 * 2 + core, v2))
-        return 0
-
-    lax.fori_loop(1, 64, give, 0)
+        to_pair[n].wait_recv()
+        pair[h] = pair[h] + amp[core, h]
+
+        def give(k, _):
+            v2 = (vert + k) % 32
+            send(pair.at[h, v2], part.at[mine], s2.at[2], r2.at[2], (h * 2 + core, v2))
+            return 0
+
+        lax.fori_loop(1 - n, 32, give, 0)
     part[mine] = pair[side, vert]
     take(up_send.at[pl.ds(0, 127)], s1.at[0])
     take(low_send.at[pl.ds(0, 15)], s1.at[1])
@@ -445,7 +442,8 @@
     take(stage_low.at[pl.ds(0, 15)], l_send)
     for copy in sent + moves:
         copy.wait_send()
-    to_pair.wait_send()
+    for copy in to_pair:
+        copy.wait_send()
     take(part.at[pl.ds(0, 63)], s2.at[2])
     take(part.at[pl.ds(0, 63)], r2.at[2])
     total = jnp.sum(part[...], axis=0)
@@ -488,7 +486,7 @@
             pltpu.VMEM((64, 8, 128), F32),
             pltpu.SemaphoreType.REGULAR,
             dma((4,)), dma((3,)),
-            dma((3,)), dma((3,)), dma((3,)), dma((3,)),
+            dma((4,)), dma((4,)), dma((3,)), dma((3,)),
             dma((CHAINS,)), dma((CHAINS,)),
             dma((CHAINS, 12)), dma((CHAINS, 12)),
             dma, dma,

time: 88.8 us -> 88.8 us (level)
  no operation moved by 1% of the time
where the time goes in v8:
time: 88.8 us; the launch traced here: 88.7 us
  Pallas kernels  87.4 us (98%)
  local copies, waits for them, and re-layouts  1.28 us (1%)
    pallas_call x1, Pallas kernels, per_device(): pl.pallas_call(kernel, out_shape=jax.ShapeDtypeStruct((8, 128), F32), in_...  87.4 us

profile of v8, /device:TPU:1, one launch (start us, length us, event | category | flops | bytes accessed | tf_op | source)
XLA Modules:
  0.0 88.7 jit_solution(2752886122753180163)
XLA Ops:
  0.0 87.4 %shard_map.91 = f32[8,128]{1,0:T(8,128)} custom-call(s32[8]{0:T(128)} %live_ref.1, s32[3,8]{1,0:T(4,128)} %bitcast.10, f32[3,8]{1,0:T(4,128)} %bitcast.11, s32[512,128]{1,0:T(8,128)} %bitcast.8, bf16[64,8,512]{2,1,0:T(8,128)(2,1)} %bitcast.7, bf16[32,8,512]{2,1,0:T(8,128)(2,1)} %bitcast.9, bf16[256,2048]{1,0:T(8,128)(2,1)} %dz_hbm.1, ...), custom_call_target="tpu_custom_call" | custom-call | flops 7000000000 | bytes 5000000 | tf_op jit(solution)/shard_map/pallas_call | solution.py:460
  87.4 1.3 %copy.11 = f32[128,8]{0,1:T(8,128)} copy(f32[128,8]{0,1:T(8,128)} %bitcast.6) | data formatting | bytes 8192
